TPU v7x, 512 devices: a whole 4x4x16 slice. The times are simulated.
512 devices in a mesh: tok: 64 (over z, y), head: 8 (over x, core).
Axes of the slice: x: 4, y: 4, z: 16, core: 2. Of those that a mesh axis runs over, the one named last changes fastest.
Arguments:
- queries: float32 [16384, 8192], P('tok', 'head'), may hold values from -200 to 200
- keys: float32 [16384, 1024], P('tok', 'head'), may hold values from -6.5 to 6.5
- values: float32 [16384, 1024], P('tok', 'head'), may hold values from -6 to 6
- cotangent: float32 [16384, 8192], P('tok', 'head'), may hold values from -6 to 6
- doc_ids: int32 [16384], P(('tok', 'head')), may hold values from 0 to 127, never falling along the last dimension, each value on 1 to 256 neighbouring positions
Outputs:
- attention_out: float32 [16384, 8192], P('tok', 'head')
- grad_queries: float32 [16384, 8192], P('tok', 'head')
- grad_keys: float32 [16384, 1024], P('tok', 'head')
- grad_values: float32 [16384, 1024], P('tok', 'head')
Inputs may be any that keep to these rules, and one draw needn't show every extreme that they name: `doc_ids`: never falling along the sequence; every document has 1 to 256 tokens.
All inputs are finite; a program needn't handle non-finite values.
Results may differ from a plain program's by a relative error of at most 0.0003.
Values sent between devices are 32-bit elements; how exact they have to be, the bound alone decides.
A program may use at most 64 MiB of HBM per device.

v0:
```python
import jax
import jax.numpy as jnp
from jax import lax
from jax.sharding import PartitionSpec as P

TASKS = 2
KBLK = 1


highest = lax.Precision.HIGHEST


def sent_to_all(array, axis):
    count = lax.axis_size(axis)
    return lax.all_to_all(
        jnp.broadcast_to(array[None], (count, *array.shape)), axis, 0, 0, tiled=True
    )


def in_order(blocks, dim):
    blocks = jnp.moveaxis(blocks, 0, dim)
    dims = blocks.shape
    return blocks.reshape(*dims[:dim], dims[dim] * dims[dim + 1], *dims[dim + 2 :])


def gather_directly(array, axis, dim):
    blocks = sent_to_all(array, axis)
    return in_order(blocks, dim)


def shifted(block, axis, distance):
    devices = range(lax.axis_size(axis))
    route = [(i - distance, i) for i in devices if i - distance in devices]
    return lax.ppermute(block, axis, route)


def allowed_pairs(query_ids, key_ids, first_key, doc_back):
    query_pos = jnp.arange(query_ids.shape[1], dtype=jnp.int32)[:, None]
    key_pos = first_key + jnp.arange(key_ids.shape[1], dtype=jnp.int32)[None, :]
    causal = key_pos <= query_pos + doc_back
    same_doc = (key_ids[:, None, :] == query_ids[:, :, None]) & (key_ids[:, None, :] > 0)
    return same_doc & causal[None]


def local_forward(query_tasks, kv_tasks, id_tasks, doc_back, head_dim):
    task_count, task_rows, width = query_tasks.shape
    group_size = width // head_dim
    score_scale = head_dim ** (-0.5)
    shaped_q = query_tasks.reshape(task_count, task_rows, group_size, head_dim)
    query_ids = id_tasks[:, doc_back:]
    tile_total = kv_tasks.shape[1] // task_rows
    start_state = (
        jnp.full((task_count, group_size, task_rows), -1e30, jnp.float32),
        jnp.zeros((task_count, group_size, task_rows), jnp.float32),
        jnp.zeros((task_count, group_size, task_rows, head_dim), jnp.float32),
    )

    def one_tile(tile_index, running):
        first_key = tile_index * task_rows
        tile_kv = lax.dynamic_slice_in_dim(kv_tasks, first_key, task_rows, 1)
        tile_ids = lax.dynamic_slice_in_dim(id_tasks, first_key, task_rows, 1)
        allowed = allowed_pairs(query_ids, tile_ids, first_key, doc_back)[:, None]

        def attend(current):
            running_max, running_sum, running_acc = current
            scores = (
                jnp.einsum("tqgd,tkd->tgqk", shaped_q, tile_kv[..., :head_dim], precision=highest)
                * score_scale
            )
            scores = jnp.where(allowed, scores, -1e30)
            new_max = jnp.maximum(running_max, jnp.max(scores, axis=-1))
            weights = jnp.where(allowed, jnp.exp(scores - new_max[..., None]), 0.0)
            factor = jnp.exp(running_max - new_max)
            new_sum = running_sum * factor + jnp.sum(weights, axis=-1)
            new_acc = running_acc * factor[..., None] + jnp.einsum(
                "tgqk,tkd->tgqd", weights, tile_kv[..., head_dim:], precision=highest
            )
            return (new_max, new_sum, new_acc)

        return lax.cond(jnp.any(allowed), attend, lambda unchanged: unchanged, running)

    final_max, final_sum, final_acc = lax.fori_loop(0, tile_total, one_tile, start_state)
    output = final_acc / final_sum[..., None]
    output = jnp.transpose(output, (0, 2, 1, 3)).reshape(
        task_count, task_rows, group_size * head_dim
    )
    logsum = jnp.transpose(final_max + jnp.log(final_sum), (0, 2, 1))
    return (output, logsum)


def local_backward(
    query_tasks, kv_tasks, id_tasks, grad_tasks, logsum, row_delta, doc_back, head_dim
):
    task_count, task_rows, width = query_tasks.shape
    group_size = width // head_dim
    score_scale = head_dim ** (-0.5)
    shaped_q = query_tasks.reshape(task_count, task_rows, group_size, head_dim)
    shaped_g = grad_tasks.reshape(task_count, task_rows, group_size, head_dim)
    logsum_t = jnp.transpose(logsum, (0, 2, 1))
    delta_t = jnp.transpose(row_delta, (0, 2, 1))
    query_ids = id_tasks[:, doc_back:]
    tile_total = kv_tasks.shape[1] // task_rows
    start_state = (jnp.zeros(shaped_q.shape, jnp.float32), jnp.zeros(kv_tasks.shape, jnp.float32))

    def one_tile(tile_index, running):
        first_key = tile_index * task_rows
        tile_kv = lax.dynamic_slice_in_dim(kv_tasks, first_key, task_rows, 1)
        tile_ids = lax.dynamic_slice_in_dim(id_tasks, first_key, task_rows, 1)
        allowed = allowed_pairs(query_ids, tile_ids, first_key, doc_back)[:, None]

        def accumulate(current):
            grad_q, grad_kv = current
            tile_keys = tile_kv[..., :head_dim]
            tile_values = tile_kv[..., head_dim:]
            scores = (
                jnp.einsum("tqgd,tkd->tgqk", shaped_q, tile_keys, precision=highest) * score_scale
            )
            scores = jnp.where(allowed, scores, -1e30)
            weights = jnp.where(allowed, jnp.exp(scores - logsum_t[..., None]), 0.0)
            grad_values = jnp.einsum("tgqk,tqgd->tkd", weights, shaped_g, precision=highest)
            grad_weights = jnp.einsum("tqgd,tkd->tgqk", shaped_g, tile_values, precision=highest)
            grad_scores = weights * (grad_weights - delta_t[..., None])
            grad_q = grad_q + score_scale * jnp.einsum(
                "tgqk,tkd->tqgd", grad_scores, tile_keys, precision=highest
            )
            grad_keys = score_scale * jnp.einsum(
                "tgqk,tqgd->tkd", grad_scores, shaped_q, precision=highest
            )
            grad_kv = lax.dynamic_update_slice_in_dim(
                grad_kv, jnp.concatenate([grad_keys, grad_values], axis=-1), first_key, 1
            )
            return (grad_q, grad_kv)

        return lax.cond(jnp.any(allowed), accumulate, lambda unchanged: unchanged, running)

    grad_q, grad_kv = lax.fori_loop(0, tile_total, one_tile, start_state)
    return (grad_q.reshape(task_count, task_rows, group_size * head_dim), grad_kv)


def output_delta(grad_tasks, out_tasks, head_dim):
    task_count, task_rows, width = grad_tasks.shape
    shaped = (task_count, task_rows, width // head_dim, head_dim)
    return jnp.sum(grad_tasks.reshape(shaped) * out_tasks.reshape(shaped), axis=-1)


def per_device(queries, keys, values, cotangent, doc_ids):
    shard_rows = keys.shape[0]
    head_dim = keys.shape[1]
    group_size = queries.shape[1] // head_dim
    task_rows = shard_rows // TASKS
    doc_back = KBLK * shard_rows
    window_rows = doc_back + task_rows
    block_ids = gather_directly(doc_ids, "head", 0)
    id_values = (block_ids + 1).astype(jnp.float32)
    keys_values = jnp.concatenate([keys, values], axis=1)
    distance = 1
    arrived = shifted((keys_values, id_values), "tok", distance)
    earlier_kv = [arrived[0]]
    earlier_ids = [arrived[1]]
    context_kv = jnp.concatenate(earlier_kv + [keys_values], axis=0)
    context_ids = jnp.concatenate(earlier_ids + [id_values], axis=0)
    kv_tasks = jnp.stack(
        [
            context_kv[part_index * task_rows : part_index * task_rows + window_rows]
            for part_index in range(TASKS)
        ]
    )
    id_tasks = jnp.stack(
        [
            context_ids[part_index * task_rows : part_index * task_rows + window_rows]
            for part_index in range(TASKS)
        ]
    )
    query_tasks = queries.reshape(TASKS, task_rows, group_size * head_dim)
    grad_tasks = cotangent.reshape(TASKS, task_rows, group_size * head_dim)
    out_tasks, logsum_tasks = local_forward(query_tasks, kv_tasks, id_tasks, doc_back, head_dim)
    delta_tasks = output_delta(grad_tasks, out_tasks, head_dim)
    dq_tasks, dkv_tasks = local_backward(
        query_tasks, kv_tasks, id_tasks, grad_tasks, logsum_tasks, delta_tasks, doc_back, head_dim
    )
    context_grad = jnp.zeros(((KBLK + 1) * shard_rows, 2 * head_dim), jnp.float32)
    for part_index in range(TASKS):
        context_grad = context_grad.at[
            part_index * task_rows : part_index * task_rows + window_rows
        ].add(dkv_tasks[part_index])
    summed = context_grad[KBLK * shard_rows :]
    distance = 1
    context_block = context_grad[
        (KBLK - distance) * shard_rows : (KBLK - distance + 1) * shard_rows
    ]
    summed = summed + shifted(context_block, "tok", -distance)
    attention_out = out_tasks.reshape(shard_rows, group_size * head_dim)
    grad_queries = dq_tasks.reshape(shard_rows, group_size * head_dim)
    return (attention_out, grad_queries, summed[:, :head_dim], summed[:, head_dim:])


def solution(mesh):
    placed = (
        P("tok", "head"),
        P("tok", "head"),
        P("tok", "head"),
        P("tok", "head"),
        P(("tok", "head")),
    )
    return jax.shard_map(
        per_device,
        mesh=mesh,
        in_specs=placed,
        out_specs=(P("tok", "head"), P("tok", "head"), P("tok", "head"), P("tok", "head")),
        check_vma=False,
    )
```

profile of v0, /device:TPU:120, one launch (start us, length us, event | category | flops | bytes accessed | tf_op | source)
XLA Modules:
  0.0 109.2 jit_solution(15159596419349901969)
XLA Ops:
  0.6 1.3 %broadcast_in_dim.112 = s32[8,1,32]{2,1,0:T(1,128)} broadcast(s32[32]{0:T(128)} %param.21), dimensions={2} | broadcast | bytes 1152 | tf_op jit(solution)/shard_map/broadcast_in_dim | solution.py:16
  1.9 4.3 %all-to-all-start = ((s32[8,1,32]{2,1,0:T(1,128)}), s32[8,1,32]{2,1,0:T(1,128)S(1)}, u32[]{:S(2)}, u32[]{:S(2)}) async-start(s32[8,1,32]{2,1,0:T(1,128)} %broadcast_in_dim.112), calls=%async_computation | async-start | bytes 8192 | tf_op jit(solution)/shard_map/all_to_all | solution.py:15
  6.2 1.0 constant_dynamic-update-slice_fusion.2
  7.1 4.2 %all-to-all-done = s32[8,1,32]{2,1,0:T(1,128)S(1)} async-done(((s32[8,1,32]{2,1,0:T(1,128)}), s32[8,1,32]{2,1,0:T(1,128)S(1)}, u32[]{:S(2)}, u32[]{:S(2)}) %all-to-all-start) | async-done | bytes 1056 | tf_op jit(solution)/shard_map/all_to_all | solution.py:15
  11.5 4.7 %collective-permute-start = (f32[256]{0:T(256)S(1)}, f32[256]{0:T(256)S(1)}, u32[]{:S(2)}, u32[]{:S(2)}) collective-permute-start(f32[256]{0:T(256)S(1)} %convert_element_type.21), channel_id=1, source_target_pairs={{0,8},{8,16},{16,24},{24,32},{32,40},{40,48},{48,56},{56,64},{64,7... | collective-permute-start | bytes 3080 | tf_op jit(solution)/shard_map/ppermute | solution.py:34
  16.2 3.5 %collective-permute-start.1 = (f32[256,256]{1,0:T(8,128)S(1)}, f32[256,256]{1,0:T(8,128)}, u32[]{:S(2)}, u32[]{:S(2)}) collective-permute-start(f32[256,256]{1,0:T(8,128)S(1)} %constant_dynamic-update-slice_fusion.1), channel_id=1, source_target_pairs={{0,8},{8,16},{16,24},{24,32},{32,40},{40,48},{48,56},{56,64},{64,7... | collective-permute-start | bytes 786440 | tf_op jit(solution)/shard_map/ppermute | solution.py:34
  19.7 1.4 %copy.62 = f32[32,8,8,128]{3,2,1,0:T(8,128)S(1)} copy(f32[32,8,8,128]{3,1,2,0:T(8,128)} %bitcast.107) | data formatting | bytes 2097152
  21.1 1.2 %copy.41 = f32[2,128,8,128]{3,1,2,0:T(8,128)} copy(f32[2,128,8,128]{3,2,1,0:T(8,128)S(1)} %bitcast.102) | data formatting | bytes 2097152 | tf_op jit(solution)/shard_map/while | solution.py:82
  22.3 0.4 copy.44
  22.7 0.9 copy-done.3
  23.7 1.3 %copy.45 = f32[2,128,8,128]{1,3,2,0:T(8,128)} copy(f32[2,128,8,128]{3,2,1,0:T(8,128)S(1)} %bitcast.100) | data formatting | bytes 2097152 | tf_op jit(solution)/shard_map/while | solution.py:136
  25.2 0.8 collective-permute-done.1
  25.9 1.0 fusion.24
  27.0 1.0 pad_maximum_fusion
  28.1 21.9 %while.34 = (s32[]{:T(128)}, f32[2,8,128]{2,1,0:T(8,128)S(1)}, f32[2,8,128]{2,1,0:T(8,128)S(1)}, f32[2,8,128,128]{3,2,1,0:T(8,128)S(1)}, f32[2,384]{1,0:T(2,128)...) while((s32[]{:T(128)}, f32[2,8,128]{2,1,0:T(8,128)S(1)}, ...), condition=%wide.region_6.7_spmd, body=%wide.region_0.6_spmd.sunk | while | flops 808079872 | bytes 6856497 | solution.py:82
  28.2 0.8 fusion.44
  29.6 5.7 %conditional.4 = ((f32[2,8,128]{2,1,0:T(8,128)S(1)}, f32[2,8,128]{2,1,0:T(8,128)S(1)}, f32[2,8,128,128]{3,2,1,0:T(8,128)S(1)})) conditional(s32[]{:T(128)} %convert_element_type.25, (f32[2,8,128]{2,1,0:T(8,128)S(1)}, f32[2,8,128]{2,1,0:T(8,128)S(1)}, f32[2,8,128,128]{3,2,1,0:T(8,128)S(1)}) %tuple.112, (pred[2,1,128,128]{2,3,0,1:T(8,128)(4,1)S(1)}, ...), branch_computations={%region_2.0_spmd, %region_3.5_spmd} | conditional | flops 807931904 | bytes 6784048 | solution.py:80
  29.7 2.4 %fusion.31 = (f32[2,8,128]{2,1,0:T(8,128)S(1)}, f32[2,8,128,128]{2,3,1,0:T(8,128)S(1)}) fusion(f32[2,128,8,128]{3,1,2,0:T(8,128)} %get-tuple-element.406, f32[2,384,256]{2,1,0:T(8,128)} %get-tuple-element.404, s32[]{:T(128)} %get-tuple-element.405, pred[2,128,128]{1,2,0:T(8,128)(4,1)S(1)} %bitcast.97), kind=kOutput, calls=%fused_computation.78 | convolution fusion | flops 403437568 | bytes 2269696 | tf_op jit(solution)/shard_map/while/body/eval_jaxpr/cond/branch_1_fun/tqgd,tkd->tgqk/dot_general | solution.py:67
  32.1 0.2 fusion.2
  32.3 3.1 %convolution_add_fusion = f32[2,8,128,128]{3,2,1,0:T(8,128)S(1)} fusion(f32[2,8,128,128]{3,2,1,0:T(8,128)S(1)} %get-tuple-element.408, f32[2,8,128,128]{2,3,1,0:T(8,128)S(1)} %get-tuple-element.553, f32[2,8,128]{2,1,0:T(8,128)S(1)} %get-tuple-element.539, f32[2,8,128]{2,1,0:T(8,128)S(1)} %max.3, pred[2,128,128]{1,2,0:T(8,128)(4,1)S(1)} %bitcast.99, ...), kind=kOutput, calls=%fused_computation | convolution fusion | flops 403701760 | bytes 3326468 | tf_op jit(solution)/shard_map/while/body/eval_jaxpr/cond/branch_1_fun/tgqk,tkd->tgqd/dot_general | solution.py:75
  35.5 0.8 fusion.44
  36.9 5.7 %conditional.4 = ((f32[2,8,128]{2,1,0:T(8,128)S(1)}, f32[2,8,128]{2,1,0:T(8,128)S(1)}, f32[2,8,128,128]{3,2,1,0:T(8,128)S(1)})) conditional(s32[]{:T(128)} %convert_element_type.25, (f32[2,8,128]{2,1,0:T(8,128)S(1)}, f32[2,8,128]{2,1,0:T(8,128)S(1)}, f32[2,8,128,128]{3,2,1,0:T(8,128)S(1)}) %tuple.112, (pred[2,1,128,128]{2,3,0,1:T(8,128)(4,1)S(1)}, ...), branch_computations={%region_2.0_spmd, %region_3.5_spmd} | conditional | flops 807931904 | bytes 6784048 | solution.py:80
  37.0 2.4 %fusion.31 = (f32[2,8,128]{2,1,0:T(8,128)S(1)}, f32[2,8,128,128]{2,3,1,0:T(8,128)S(1)}) fusion(f32[2,128,8,128]{3,1,2,0:T(8,128)} %get-tuple-element.406, f32[2,384,256]{2,1,0:T(8,128)} %get-tuple-element.404, s32[]{:T(128)} %get-tuple-element.405, pred[2,128,128]{1,2,0:T(8,128)(4,1)S(1)} %bitcast.97), kind=kOutput, calls=%fused_computation.78 | convolution fusion | flops 403437568 | bytes 2269696 | tf_op jit(solution)/shard_map/while/body/eval_jaxpr/cond/branch_1_fun/tqgd,tkd->tgqk/dot_general | solution.py:67
  39.4 0.2 fusion.2
  39.6 3.1 %convolution_add_fusion = f32[2,8,128,128]{3,2,1,0:T(8,128)S(1)} fusion(f32[2,8,128,128]{3,2,1,0:T(8,128)S(1)} %get-tuple-element.408, f32[2,8,128,128]{2,3,1,0:T(8,128)S(1)} %get-tuple-element.553, f32[2,8,128]{2,1,0:T(8,128)S(1)} %get-tuple-element.539, f32[2,8,128]{2,1,0:T(8,128)S(1)} %max.3, pred[2,128,128]{1,2,0:T(8,128)(4,1)S(1)} %bitcast.99, ...), kind=kOutput, calls=%fused_computation | convolution fusion | flops 403701760 | bytes 3326468 | tf_op jit(solution)/shard_map/while/body/eval_jaxpr/cond/branch_1_fun/tgqk,tkd->tgqd/dot_general | solution.py:75
  42.8 0.8 fusion.44
  44.3 5.7 %conditional.4 = ((f32[2,8,128]{2,1,0:T(8,128)S(1)}, f32[2,8,128]{2,1,0:T(8,128)S(1)}, f32[2,8,128,128]{3,2,1,0:T(8,128)S(1)})) conditional(s32[]{:T(128)} %convert_element_type.25, (f32[2,8,128]{2,1,0:T(8,128)S(1)}, f32[2,8,128]{2,1,0:T(8,128)S(1)}, f32[2,8,128,128]{3,2,1,0:T(8,128)S(1)}) %tuple.112, (pred[2,1,128,128]{2,3,0,1:T(8,128)(4,1)S(1)}, ...), branch_computations={%region_2.0_spmd, %region_3.5_spmd} | conditional | flops 807931904 | bytes 6784048 | solution.py:80
  44.3 2.4 %fusion.31 = (f32[2,8,128]{2,1,0:T(8,128)S(1)}, f32[2,8,128,128]{2,3,1,0:T(8,128)S(1)}) fusion(f32[2,128,8,128]{3,1,2,0:T(8,128)} %get-tuple-element.406, f32[2,384,256]{2,1,0:T(8,128)} %get-tuple-element.404, s32[]{:T(128)} %get-tuple-element.405, pred[2,128,128]{1,2,0:T(8,128)(4,1)S(1)} %bitcast.97), kind=kOutput, calls=%fused_computation.78 | convolution fusion | flops 403437568 | bytes 2269696 | tf_op jit(solution)/shard_map/while/body/eval_jaxpr/cond/branch_1_fun/tqgd,tkd->tgqk/dot_general | solution.py:67
  46.7 0.2 fusion.2
  46.9 3.1 %convolution_add_fusion = f32[2,8,128,128]{3,2,1,0:T(8,128)S(1)} fusion(f32[2,8,128,128]{3,2,1,0:T(8,128)S(1)} %get-tuple-element.408, f32[2,8,128,128]{2,3,1,0:T(8,128)S(1)} %get-tuple-element.553, f32[2,8,128]{2,1,0:T(8,128)S(1)} %get-tuple-element.539, f32[2,8,128]{2,1,0:T(8,128)S(1)} %max.3, pred[2,128,128]{1,2,0:T(8,128)(4,1)S(1)} %bitcast.99, ...), kind=kOutput, calls=%fused_computation | convolution fusion | flops 403701760 | bytes 3326468 | tf_op jit(solution)/shard_map/while/body/eval_jaxpr/cond/branch_1_fun/tgqk,tkd->tgqd/dot_general | solution.py:75
  50.1 3.0 %fusion.22 = (f32[2,128,8]{2,1,0:T(8,128)S(1)}, f32[2,8,128,128]{3,1,2,0:T(8,128)}) fusion(f32[2,8,128]{1,2,0:T(8,128)S(1)} %copy.42, f32[2,8,128,128]{3,2,1,0:T(8,128)S(1)} %get-tuple-element.453, f32[2,128,8,128]{3,2,1,0:T(8,128)} %bitcast.101), kind=kLoop, calls=%fused_computation.52 | loop fusion | flops 784384 | bytes 3162112 | tf_op jit(solution)/shard_map/reduce_sum | solution.py:143
  53.2 1.1 %broadcast_in_dim.113 = f32[2,128,8,128]{3,1,2,0:T(8,128)} broadcast(f32[]{:T(128)} %constant.190.clone.1), dimensions={} | broadcast | bytes 1048580 | tf_op jit(solution)/shard_map/broadcast_in_dim | solution.py:103
  54.3 1.0 broadcast_in_dim.114
  55.3 39.5 %while.35 = (s32[]{:T(128)}, f32[2,128,8,128]{3,1,2,0:T(8,128)}, f32[2,384,256]{1,2,0:T(8,128)}, f32[2,384]{1,0:T(2,128)S(1)}, f32[2,128]{1,0:T(2,128)S(1)}, /*i...) while((s32[]{:T(128)}, f32[2,128,8,128]{3,1,2,0:T(8,128)}, ...), condition=%wide.region_12.13_spmd, body=%wide.region_8.12_spmd.sunk | while | flops 2015609344 | bytes 18080140 | solution.py:136
  55.4 0.8 fusion.45
  56.8 11.6 %conditional.5 = ((f32[2,128,8,128]{3,1,2,0:T(8,128)}, f32[2,384,256]{1,2,0:T(8,128)})) conditional(s32[]{:T(128)} %convert_element_type.26, (f32[2,128,8,128]{3,1,2,0:T(8,128)}, f32[2,384,256]{1,2,0:T(8,128)}) %tuple.118, (pred[2,1,128,128]{2,3,0,1:T(8,128)(4,1)S(1)}, f32[2,384,256]{2,1,0:T(8,128)}, s32[]{:T(128)}, ...), branch_computations={%region_10.10_spmd, %region_11.11_spmd} | conditional | flops 2015461376 | bytes 18007658 | solution.py:134
  56.8 2.1 %fusion.17 = f32[2,8,128,128]{2,3,1,0:T(8,128)S(1)} fusion(f32[2,128,8,128]{1,3,2,0:T(8,128)S(1)} %get-tuple-element.425, f32[2,8,128]{2,1,0:T(8,128)S(1)} %get-tuple-element.426, pred[2,128,128]{1,2,0:T(8,128)(4,1)S(1)} %bitcast.106, f32[2,384,256]{2,1,0:T(8,128)} %get-tuple-element.423, s32[]{:T(128)} %get-tuple-element.424), kind=kOutput, calls=%fused_computation.33 | convolution fusion | flops 403701760 | bytes 2269696 | tf_op jit(solution)/shard_map/while/body/eval_jaxpr/cond/branch_1_fun/tqgd,tkd->tgqk/dot_general | solution.py:116
  58.9 2.3 %fusion.12 = f32[2,8,128,128]{2,3,1,0:T(8,128)S(1)} fusion(f32[2,8,128,128]{2,3,1,0:T(8,128)S(1)} %fusion.17, f32[2,128,8,128]{1,3,2,0:T(8,128)} %get-tuple-element.427, f32[2,8,128]{2,1,0:T(8,128)S(1)} %get-tuple-element.428, f32[2,384,256]{2,1,0:T(8,128)} %get-tuple-element.423, s32[]{:T(128)} %get-tuple-element.424, s32[]{:T(128)S(6)} %add.160), kind=kOutput, calls=%fused_computation.27 | convolution fusion | flops 403177472 | bytes 3285508 | tf_op jit(solution)/shard_map/while/body/eval_jaxpr/cond/branch_1_fun/tqgd,tkd->tgqk/dot_general | solution.py:121
  61.2 1.2 %fusion.18 = f32[2,128,128]{1,2,0:T(8,128)S(1)} fusion(f32[2,8,128,128]{2,3,1,0:T(8,128)S(1)} %fusion.12, f32[2,128,8,128]{1,3,2,0:T(8,128)S(1)} %get-tuple-element.425), kind=kOutput, calls=%fused_computation.36 | convolution fusion | flops 402685952 | bytes 2228224 | tf_op jit(solution)/shard_map/while/body/eval_jaxpr/cond/branch_1_fun/tgqk,tqgd->tkd/dot_general | solution.py:126
  62.5 1.1 %convolution_bitcast_fusion.1 = f32[2,128,128]{1,2,0:T(8,128)S(1)} fusion(f32[2,8,128,128]{2,3,1,0:T(8,128)S(1)} %fusion.17, f32[2,128,8,128]{1,3,2,0:T(8,128)S(1)} %copy-done), kind=kOutput, calls=%fused_computation.34 | convolution fusion | flops 402653184 | bytes 2228224 | tf_op jit(solution)/shard_map/while/body/eval_jaxpr/cond/branch_1_fun/tgqk,tqgd->tkd/dot_general | solution.py:120
  63.6 0.7 maximum_dynamic-update-slice_fusion
  64.4 4.1 %fusion.10 = f32[2,128,8,128]{3,1,2,0:T(8,128)} fusion(f32[2,128,8,128]{3,1,2,0:T(8,128)} %get-tuple-element.421, f32[2,8,128,128]{2,3,1,0:T(8,128)S(1)} %fusion.12, f32[2,384,256]{2,1,0:T(8,128)} %get-tuple-element.423, s32[]{:T(128)} %get-tuple-element.424), kind=kOutput, calls=%fused_computation.24 | convolution fusion | flops 403177472 | bytes 3277312 | tf_op jit(solution)/shard_map/while/body/eval_jaxpr/cond/branch_1_fun/tgqk,tkd->tqgd/dot_general | solution.py:123
  68.5 0.8 fusion.45
  70.0 11.6 %conditional.5 = ((f32[2,128,8,128]{3,1,2,0:T(8,128)}, f32[2,384,256]{1,2,0:T(8,128)})) conditional(s32[]{:T(128)} %convert_element_type.26, (f32[2,128,8,128]{3,1,2,0:T(8,128)}, f32[2,384,256]{1,2,0:T(8,128)}) %tuple.118, (pred[2,1,128,128]{2,3,0,1:T(8,128)(4,1)S(1)}, f32[2,384,256]{2,1,0:T(8,128)}, s32[]{:T(128)}, ...), branch_computations={%region_10.10_spmd, %region_11.11_spmd} | conditional | flops 2015461376 | bytes 18007658 | solution.py:134
  70.0 2.1 %fusion.17 = f32[2,8,128,128]{2,3,1,0:T(8,128)S(1)} fusion(f32[2,128,8,128]{1,3,2,0:T(8,128)S(1)} %get-tuple-element.425, f32[2,8,128]{2,1,0:T(8,128)S(1)} %get-tuple-element.426, pred[2,128,128]{1,2,0:T(8,128)(4,1)S(1)} %bitcast.106, f32[2,384,256]{2,1,0:T(8,128)} %get-tuple-element.423, s32[]{:T(128)} %get-tuple-element.424), kind=kOutput, calls=%fused_computation.33 | convolution fusion | flops 403701760 | bytes 2269696 | tf_op jit(solution)/shard_map/while/body/eval_jaxpr/cond/branch_1_fun/tqgd,tkd->tgqk/dot_general | solution.py:116
  72.1 2.3 %fusion.12 = f32[2,8,128,128]{2,3,1,0:T(8,128)S(1)} fusion(f32[2,8,128,128]{2,3,1,0:T(8,128)S(1)} %fusion.17, f32[2,128,8,128]{1,3,2,0:T(8,128)} %get-tuple-element.427, f32[2,8,128]{2,1,0:T(8,128)S(1)} %get-tuple-element.428, f32[2,384,256]{2,1,0:T(8,128)} %get-tuple-element.423, s32[]{:T(128)} %get-tuple-element.424, s32[]{:T(128)S(6)} %add.160), kind=kOutput, calls=%fused_computation.27 | convolution fusion | flops 403177472 | bytes 3285508 | tf_op jit(solution)/shard_map/while/body/eval_jaxpr/cond/branch_1_fun/tqgd,tkd->tgqk/dot_general | solution.py:121
  74.4 1.1 %fusion.18 = f32[2,128,128]{1,2,0:T(8,128)S(1)} fusion(f32[2,8,128,128]{2,3,1,0:T(8,128)S(1)} %fusion.12, f32[2,128,8,128]{1,3,2,0:T(8,128)S(1)} %get-tuple-element.425), kind=kOutput, calls=%fused_computation.36 | convolution fusion | flops 402685952 | bytes 2228224 | tf_op jit(solution)/shard_map/while/body/eval_jaxpr/cond/branch_1_fun/tgqk,tqgd->tkd/dot_general | solution.py:126
  75.6 1.1 %convolution_bitcast_fusion.1 = f32[2,128,128]{1,2,0:T(8,128)S(1)} fusion(f32[2,8,128,128]{2,3,1,0:T(8,128)S(1)} %fusion.17, f32[2,128,8,128]{1,3,2,0:T(8,128)S(1)} %copy-done), kind=kOutput, calls=%fused_computation.34 | convolution fusion | flops 402653184 | bytes 2228224 | tf_op jit(solution)/shard_map/while/body/eval_jaxpr/cond/branch_1_fun/tgqk,tqgd->tkd/dot_general | solution.py:120
  76.8 0.8 maximum_dynamic-update-slice_fusion
  77.5 4.1 %fusion.10 = f32[2,128,8,128]{3,1,2,0:T(8,128)} fusion(f32[2,128,8,128]{3,1,2,0:T(8,128)} %get-tuple-element.421, f32[2,8,128,128]{2,3,1,0:T(8,128)S(1)} %fusion.12, f32[2,384,256]{2,1,0:T(8,128)} %get-tuple-element.423, s32[]{:T(128)} %get-tuple-element.424), kind=kOutput, calls=%fused_computation.24 | convolution fusion | flops 403177472 | bytes 3277312 | tf_op jit(solution)/shard_map/while/body/eval_jaxpr/cond/branch_1_fun/tgqk,tkd->tqgd/dot_general | solution.py:123
  81.7 0.8 fusion.45
  83.1 11.7 %conditional.5 = ((f32[2,128,8,128]{3,1,2,0:T(8,128)}, f32[2,384,256]{1,2,0:T(8,128)})) conditional(s32[]{:T(128)} %convert_element_type.26, (f32[2,128,8,128]{3,1,2,0:T(8,128)}, f32[2,384,256]{1,2,0:T(8,128)}) %tuple.118, (pred[2,1,128,128]{2,3,0,1:T(8,128)(4,1)S(1)}, f32[2,384,256]{2,1,0:T(8,128)}, s32[]{:T(128)}, ...), branch_computations={%region_10.10_spmd, %region_11.11_spmd} | conditional | flops 2015461376 | bytes 18007658 | solution.py:134
  83.1 2.1 %fusion.17 = f32[2,8,128,128]{2,3,1,0:T(8,128)S(1)} fusion(f32[2,128,8,128]{1,3,2,0:T(8,128)S(1)} %get-tuple-element.425, f32[2,8,128]{2,1,0:T(8,128)S(1)} %get-tuple-element.426, pred[2,128,128]{1,2,0:T(8,128)(4,1)S(1)} %bitcast.106, f32[2,384,256]{2,1,0:T(8,128)} %get-tuple-element.423, s32[]{:T(128)} %get-tuple-element.424), kind=kOutput, calls=%fused_computation.33 | convolution fusion | flops 403701760 | bytes 2269696 | tf_op jit(solution)/shard_map/while/body/eval_jaxpr/cond/branch_1_fun/tqgd,tkd->tgqk/dot_general | solution.py:116
  85.2 2.3 %fusion.12 = f32[2,8,128,128]{2,3,1,0:T(8,128)S(1)} fusion(f32[2,8,128,128]{2,3,1,0:T(8,128)S(1)} %fusion.17, f32[2,128,8,128]{1,3,2,0:T(8,128)} %get-tuple-element.427, f32[2,8,128]{2,1,0:T(8,128)S(1)} %get-tuple-element.428, f32[2,384,256]{2,1,0:T(8,128)} %get-tuple-element.423, s32[]{:T(128)} %get-tuple-element.424, s32[]{:T(128)S(6)} %add.160), kind=kOutput, calls=%fused_computation.27 | convolution fusion | flops 403177472 | bytes 3285508 | tf_op jit(solution)/shard_map/while/body/eval_jaxpr/cond/branch_1_fun/tqgd,tkd->tgqk/dot_general | solution.py:121
  87.6 1.2 %fusion.18 = f32[2,128,128]{1,2,0:T(8,128)S(1)} fusion(f32[2,8,128,128]{2,3,1,0:T(8,128)S(1)} %fusion.12, f32[2,128,8,128]{1,3,2,0:T(8,128)S(1)} %get-tuple-element.425), kind=kOutput, calls=%fused_computation.36 | convolution fusion | flops 402685952 | bytes 2228224 | tf_op jit(solution)/shard_map/while/body/eval_jaxpr/cond/branch_1_fun/tgqk,tqgd->tkd/dot_general | solution.py:126
  88.8 1.1 %convolution_bitcast_fusion.1 = f32[2,128,128]{1,2,0:T(8,128)S(1)} fusion(f32[2,8,128,128]{2,3,1,0:T(8,128)S(1)} %fusion.17, f32[2,128,8,128]{1,3,2,0:T(8,128)S(1)} %copy-done), kind=kOutput, calls=%fused_computation.34 | convolution fusion | flops 402653184 | bytes 2228224 | tf_op jit(solution)/shard_map/while/body/eval_jaxpr/cond/branch_1_fun/tgqk,tqgd->tkd/dot_general | solution.py:120
  89.9 0.8 maximum_dynamic-update-slice_fusion
  90.7 4.1 %fusion.10 = f32[2,128,8,128]{3,1,2,0:T(8,128)} fusion(f32[2,128,8,128]{3,1,2,0:T(8,128)} %get-tuple-element.421, f32[2,8,128,128]{2,3,1,0:T(8,128)S(1)} %fusion.12, f32[2,384,256]{2,1,0:T(8,128)} %get-tuple-element.423, s32[]{:T(128)} %get-tuple-element.424), kind=kOutput, calls=%fused_computation.24 | convolution fusion | flops 403177472 | bytes 3277312 | tf_op jit(solution)/shard_map/while/body/eval_jaxpr/cond/branch_1_fun/tgqk,tkd->tqgd/dot_general | solution.py:123
  94.8 1.4 %copy.48 = f32[2,384,256]{2,1,0:T(8,128)S(1)} copy(f32[2,384,256]{1,2,0:T(8,128)} %get-tuple-element.457) | data formatting | bytes 1572864 | tf_op jit(solution)/shard_map/while | solution.py:136
  96.4 1.9 %collective-permute-start.2 = (f32[256,256]{1,0:T(8,128)S(1)}, f32[256,256]{1,0:T(8,128)S(1)}, u32[]{:S(2)}, u32[]{:S(2)}) collective-permute-start(f32[256,256]{1,0:T(8,128)S(1)} %slice.105), channel_id=1, source_target_pairs={{8,0},{16,8},{24,16},{32,24},{40,32},{48,40},{56,48},{64,56},{72,6... | collective-permute-start | bytes 786440 | tf_op jit(solution)/shard_map/ppermute | solution.py:34
  98.3 1.9 %copy.47 = f32[2,128,8,128]{3,2,1,0:T(8,128)S(1)} copy(f32[2,128,8,128]{3,1,2,0:T(8,128)} %get-tuple-element.456) | data formatting | bytes 2097152 | tf_op jit(solution)/shard_map/while | solution.py:136
  100.2 1.8 %copy_bitcast_fusion = (f32[256,1024]{1,0:T(8,128)}, f32[256,1024]{1,0:T(8,128)}) fusion(f32[32,8,8,128]{3,2,1,0:T(8,128)S(1)} %bitcast.105, f32[32,8,8,128]{3,2,1,0:T(8,128)S(1)} %bitcast.104), kind=kLoop, calls=%fused_computation.49 | loop fusion | bytes 4194304 | tf_op jit(solution)/shard_map/reshape;reshape | solution.py:193
  102.0 6.4 %collective-permute-done.2 = f32[256,256]{1,0:T(8,128)S(1)} collective-permute-done((f32[256,256]{1,0:T(8,128)S(1)}, f32[256,256]{1,0:T(8,128)S(1)}, u32[]{:S(2)}, u32[]{:S(2)}) %collective-permute-start.2) | collective-permute-done | bytes 262176 | tf_op jit(solution)/shard_map/ppermute | solution.py:34
  108.4 0.7 fusion.32
  (64 shorter events, 1.7 us)
Async XLA Ops:
  1.9 9.5 %all-to-all-start = ((s32[8,1,32]{2,1,0:T(1,128)}), s32[8,1,32]{2,1,0:T(1,128)S(1)}, u32[]{:S(2)}, u32[]{:S(2)}) async-start(s32[8,1,32]{2,1,0:T(1,128)} %broadcast_in_dim.112), calls=%async_computation | async-start | bytes 8192 | tf_op jit(solution)/shard_map/all_to_all | solution.py:15
  6.2 10.0 %copy-start.4 = (f32[256,128]{1,0:T(8,128)S(1)}, f32[256,128]{1,0:T(8,128)}, u32[]{:S(2)}) copy-start(f32[256,128]{1,0:T(8,128)} %param.19) | copy-start | bytes 393220
  11.5 13.6 %collective-permute-start = (f32[256]{0:T(256)S(1)}, f32[256]{0:T(256)S(1)}, u32[]{:S(2)}, u32[]{:S(2)}) collective-permute-start(f32[256]{0:T(256)S(1)} %convert_element_type.21), channel_id=1, source_target_pairs={{0,8},{8,16},{16,24},{24,32},{32,40},{40,48},{48,56},{56,64},{64,7... | collective-permute-start | bytes 3080 | tf_op jit(solution)/shard_map/ppermute | solution.py:34
  16.2 9.7 %collective-permute-start.1 = (f32[256,256]{1,0:T(8,128)S(1)}, f32[256,256]{1,0:T(8,128)}, u32[]{:S(2)}, u32[]{:S(2)}) collective-permute-start(f32[256,256]{1,0:T(8,128)S(1)} %constant_dynamic-update-slice_fusion.1), channel_id=1, source_target_pairs={{0,8},{8,16},{16,24},{24,32},{32,40},{40,48},{48,56},{56,64},{64,7... | collective-permute-start | bytes 786440 | tf_op jit(solution)/shard_map/ppermute | solution.py:34
  22.3 1.2 %copy-start.3 = (f32[256,1024]{1,0:T(8,128)S(1)}, f32[256,1024]{1,0:T(8,128)}, u32[]{:S(2)}) copy-start(f32[256,1024]{1,0:T(8,128)} %param.20) | copy-start | bytes 3145732
  23.7 1.4 %copy-start.1 = (f32[32,8,8,128]{3,2,1,0:T(8,128)}, f32[32,8,8,128]{3,2,1,0:T(8,128)S(1)}, u32[]{:S(2)}) copy-start(f32[32,8,8,128]{3,2,1,0:T(8,128)S(1)} %copy.64) | copy-start | bytes 3145732
  61.2 1.2 %copy-start = (f32[2,128,8,128]{1,3,2,0:T(8,128)S(1)}, f32[2,128,8,128]{1,3,2,0:T(8,128)}, u32[]{:S(2)}) copy-start(f32[2,128,8,128]{1,3,2,0:T(8,128)} %get-tuple-element.427) | copy-start | bytes 3145732 | tf_op jit(solution)/shard_map/while/body/eval_jaxpr/cond
  74.4 1.2 %copy-start = (f32[2,128,8,128]{1,3,2,0:T(8,128)S(1)}, f32[2,128,8,128]{1,3,2,0:T(8,128)}, u32[]{:S(2)}) copy-start(f32[2,128,8,128]{1,3,2,0:T(8,128)} %get-tuple-element.427) | copy-start | bytes 3145732 | tf_op jit(solution)/shard_map/while/body/eval_jaxpr/cond
  87.5 1.2 %copy-start = (f32[2,128,8,128]{1,3,2,0:T(8,128)S(1)}, f32[2,128,8,128]{1,3,2,0:T(8,128)}, u32[]{:S(2)}) copy-start(f32[2,128,8,128]{1,3,2,0:T(8,128)} %get-tuple-element.427) | copy-start | bytes 3145732 | tf_op jit(solution)/shard_map/while/body/eval_jaxpr/cond
  96.4 12.0 %collective-permute-start.2 = (f32[256,256]{1,0:T(8,128)S(1)}, f32[256,256]{1,0:T(8,128)S(1)}, u32[]{:S(2)}, u32[]{:S(2)}) collective-permute-start(f32[256,256]{1,0:T(8,128)S(1)} %slice.105), channel_id=1, source_target_pairs={{8,0},{16,8},{24,16},{32,24},{40,32},{48,40},{56,48},{64,56},{72,6... | collective-permute-start | bytes 786440 | tf_op jit(solution)/shard_map/ppermute | solution.py:34
  98.3 1.9 %copy-start.2 = (f32[2,8,128,128]{3,1,2,0:T(8,128)S(1)}, f32[2,8,128,128]{3,1,2,0:T(8,128)}, u32[]{:S(2)}) copy-start(f32[2,8,128,128]{3,1,2,0:T(8,128)} %get-tuple-element.551) | copy-start | bytes 3145732
where the time goes:
time: 110 us; the launch traced here: 109 us
  matrix products  48.6 us (44%)
  local copies, waits for them, and re-layouts  16.2 us (15%)
  starting transfers between devices  14.4 us (13%)
  other arithmetic  13.4 us (12%)
  waiting for transfers between devices  11.4 us (10%)
  loops' own time  4.33 us (4%)
    dot_general x3, matrix products, accumulate(): jnp.einsum('tgqk,tkd->tqgd', grad_scores, tile_keys, precision=highest)  12.2 us
    ppermute x3, starting transfers between devices, shifted(): return lax.ppermute(block, axis, route)  10.1 us
    dot_general x3, matrix products, attend(): jnp.einsum('tgqk,tkd->tgqd', weights, tile_kv[..., head_dim:], precision=...  9.16 us
    dot_general x3, matrix products, attend(): jnp.einsum('tqgd,tkd->tgqk', shaped_q, tile_kv[..., :head_dim], precision...  7.17 us
    ppermute x3, waiting for transfers between devices, shifted(): return lax.ppermute(block, axis, route)  7.15 us
    dot_general x3, matrix products, accumulate(): jnp.einsum('tqgd,tkd->tgqk', shaped_g, tile_values, precision=highest)  6.95 us
    dot_general x3, matrix products, accumulate(): jnp.einsum('tqgd,tkd->tgqk', shaped_q, tile_keys, precision=highest)  6.23 us
    while x5, local copies, waits for them, and re-layouts, local_backward(): grad_q, grad_kv = lax.fori_loop(0, tile_total, one_tile, start_state)  5.08 us
  transfers between devices with their start and end apart: 4, of which 3 were waited for; matrix products, arithmetic and copies ran while one was open for 8% of the time, Pallas kernels for 0%

commit v1 on v0

v1 whole, which is shorter than its diff:
```python
import functools
import math

import jax
import jax.numpy as jnp
from jax import lax
from jax.experimental import pallas as pl
from jax.experimental.pallas import tpu as pltpu
from jax.sharding import PartitionSpec as P

HEAD_DIM = 128
TILE = 128
PAIRS = 4
TASKS = 2
IDS = 32
MESH = pl.DeviceIdType.MESH
SCORE_SCALE = HEAD_DIM**-0.5
LOG2E = math.log2(math.e)
NEG = -1e30

f32 = jnp.float32
bf16 = jnp.bfloat16


def parts2(x):
    high = x.astype(bf16)
    low = (x - high.astype(f32)).astype(bf16)
    return high, low


def parts3(x):
    high = x.astype(bf16)
    rest = x - high.astype(f32)
    mid = rest.astype(bf16)
    low = (rest - mid.astype(f32)).astype(bf16)
    return high, mid, low


def lanes(*xs):
    return jnp.concatenate(xs, axis=1)


def rows(*xs):
    return jnp.concatenate(xs, axis=0)


def dot_nn(a, b):
    return lax.dot_general(a, b, (((1,), (0,)), ((), ())), preferred_element_type=f32)


def dot_nt(a, b):
    return lax.dot_general(a, b, (((1,), (1,)), ((), ())), preferred_element_type=f32)


def kernel(
    tok_count,
    head_count,
    q_hbm,
    k_hbm,
    v_hbm,
    g_hbm,
    ids_ref,
    o_ref,
    dq_ref,
    dk_ref,
    dv_ref,
    qf,
    gf,
    k_own,
    v_own,
    k_prev,
    v_prev,
    gk_out,
    gv_out,
    gk_in,
    gv_in,
    id_mine,
    id_got,
    id_own,
    id_prev,
    bias,
    qp,
    gp,
    kc,
    vc,
    kt,
    vt,
    s_own,
    dp_own,
    pf,
    p1,
    p2,
    ds1,
    ds2,
    acc_k,
    acc_v,
    local_sem,
    send_sem,
    recv_sem,
    id_send_sem,
    id_recv_sem,
):
    tok = lax.axis_index("tok")
    head = lax.axis_index("head")
    nxt = (lax.rem(tok + 1, tok_count), head)
    prv = (lax.rem(tok + tok_count - 1, tok_count), head)
    peers = [(tok, lax.rem(head + j, head_count)) for j in range(1, head_count)]

    loads = [
        pltpu.make_async_copy(src, dst, local_sem.at[i])
        for i, (src, dst) in enumerate(
            [(k_hbm, k_own), (v_hbm, v_own), (q_hbm, qf), (g_hbm, gf)]
        )
    ]
    for load in loads:
        load.start()

    barrier = pltpu.get_barrier_semaphore()
    for device in [nxt, prv, *peers]:
        pl.semaphore_signal(barrier, inc=1, device_id=device, device_id_type=MESH)

    spread = (
        lax.broadcasted_iota(jnp.int32, (IDS, TILE), 1) % IDS
        == lax.broadcasted_iota(jnp.int32, (IDS, TILE), 0)
    )
    ids = jnp.broadcast_to(ids_ref[...].astype(f32), (8, IDS)).astype(bf16)
    id_mine[...] = dot_nn(ids, jnp.where(spread, 1.0, 0.0).astype(bf16))
    id_got[head] = id_mine[...]

    pl.semaphore_wait(barrier, head_count + 1)

    id_copies = [
        pltpu.make_async_remote_copy(
            src_ref=id_mine,
            dst_ref=id_got.at[head],
            send_sem=id_send_sem.at[j],
            recv_sem=id_recv_sem.at[j],
            device_id=device,
            device_id_type=MESH,
        )
        for j, device in enumerate(peers)
    ]
    for copy in id_copies:
        copy.start()

    def to(device, i, src, dst):
        return pltpu.make_async_remote_copy(
            src_ref=src,
            dst_ref=dst,
            send_sem=send_sem.at[i],
            recv_sem=recv_sem.at[i],
            device_id=device,
            device_id_type=MESH,
        )

    send_k = to(nxt, 0, k_hbm, k_prev)
    send_v = to(nxt, 1, v_hbm, v_prev)
    send_id = to(nxt, 2, id_own, id_prev)
    send_gk = to(prv, 3, gk_out, gk_in)
    send_gv = to(prv, 4, gv_out, gv_in)
    send_k.start()

    def pack_k(k, base):
        a, b, c = parts3(k)
        kc[base : base + 2 * TILE] = lanes(a, a, b, b, c, a)
        kt[:, base : base + 2 * TILE] = rows(*parts2(k.T))

    def pack_v(v, base):
        a, b = parts2(v)
        vc[base : base + 2 * TILE] = lanes(a, a, b, b)
        vt[:, base : base + 2 * TILE] = rows(*parts2(v.T))

    loads[0].wait()
    loads[1].wait()
    pack_k(k_own[...], 2 * TILE)
    pack_v(v_own[...], 2 * TILE)
    loads[2].wait()
    loads[3].wait()

    def q_pack(t, pair):
        a, b, c = (qp[t, pair, :, i * TILE : (i + 1) * TILE] for i in range(3))
        return lanes(a, b, a, b, a, c)

    def g_pack(t, pair):
        g = gp[t, pair]
        return lanes(g, g)

    def own_scores(pair, _):
        columns = pl.ds(pl.multiple_of(pair * 2 * TILE, 2 * TILE), 2 * TILE)
        for t in range(TASKS):
            of_task = slice(t * TILE, (t + 1) * TILE)
            q = qf[of_task, columns] * (SCORE_SCALE * LOG2E)
            qp[t, pair] = lanes(*parts3(rows(q[:, :TILE], q[:, TILE:])))
            g = gf[of_task, columns]
            gp[t, pair] = lanes(*parts2(rows(g[:, :TILE], g[:, TILE:])))
            own = slice(2 * TILE, (3 + t) * TILE)
            kept = slice(t * TILE, (1 + 2 * t) * TILE)
            s_own[pair, kept] = dot_nt(kc[own], q_pack(t, pair))
            dp_own[pair, kept] = dot_nt(vc[own], g_pack(t, pair))
        return 0

    lax.fori_loop(0, PAIRS, own_scores, 0)

    for copy in id_copies:
        copy.wait_recv()
    lane_group = lax.broadcasted_iota(jnp.int32, (8, TILE), 1) // IDS
    for t in range(TASKS):
        row = id_got[4 * t]
        for j in range(1, TILE // IDS):
            row = jnp.where(lane_group == j, id_got[4 * t + j], row)
        id_own[t] = row
    send_id.start()
    send_v.start()

    send_id.wait_recv()
    id_rows = [jnp.where(tok == 0, -1.0, id_prev[t]) for t in range(TASKS)]
    id_rows += [id_own[t] for t in range(TASKS)]
    wide = [jnp.broadcast_to(r[0:1], (TILE, TILE)) for r in id_rows]
    causal = lax.broadcasted_iota(jnp.int32, (TILE, TILE), 0) <= lax.broadcasted_iota(
        jnp.int32, (TILE, TILE), 1
    )
    for t in range(TASKS):
        for j in range(3):
            allowed = wide[t + j].T == wide[2 + t]
            if j == 2:
                allowed = allowed & causal
            bias[t, j * TILE : (j + 1) * TILE] = jnp.where(allowed, 0.0, NEG)

    send_k.wait_recv()
    pack_k(k_prev[...], 0)

    acc_k[...] = jnp.zeros_like(acc_k)
    acc_v[...] = jnp.zeros_like(acc_v)

    def probs(pair, _):
        for t in range(TASKS):
            before = slice(t * TILE, 2 * TILE)
            kept = slice(t * TILE, (1 + 2 * t) * TILE)
            b = bias[t]
            s = rows(dot_nt(kc[before], q_pack(t, pair)), s_own[pair, kept]) + lanes(b, b)
            weights = jnp.exp2(s - jnp.max(s, axis=0, keepdims=True))
            p = weights * (1.0 / jnp.sum(weights, axis=0, keepdims=True))
            pf[t, pair] = p
            high, low = parts2(p)
            p1[t, pair] = high
            p2[t, pair] = low
            g = gp[t, pair]
            ahead = (2 - t) * TILE
            acc_v[before] += dot_nn(lanes(high[:ahead], low[:ahead]), rows(g, g))
        return 0

    lax.fori_loop(0, PAIRS, probs, 0)
    gv_out[...] = acc_v[: 2 * TILE, :TILE] + acc_v[: 2 * TILE, TILE:]
    send_gv.start()

    def own_values(pair, _):
        for t in range(TASKS):
            own = slice(2 * TILE, (3 + t) * TILE)
            ahead = (2 - t) * TILE
            g = gp[t, pair]
            acc_v[own] += dot_nn(lanes(p1[t, pair, ahead:], p2[t, pair, ahead:]), rows(g, g))
        return 0

    lax.fori_loop(0, PAIRS, own_values, 0)

    send_v.wait_recv()
    pack_v(v_prev[...], 0)

    def grads(pair, _):
        for t in range(TASKS):
            before = slice(t * TILE, 2 * TILE)
            kept = slice(t * TILE, (1 + 2 * t) * TILE)
            dp = rows(dot_nt(vc[before], g_pack(t, pair)), dp_own[pair, kept])
            p = pf[t, pair]
            delta = jnp.sum(p * dp, axis=0, keepdims=True)
            high, low = parts2(p * (dp - delta))
            ds1[t, pair] = high
            ds2[t, pair] = low
            q = qp[t, pair, :, : 2 * TILE]
            ahead = (2 - t) * TILE
            acc_k[before] += dot_nn(lanes(high[:ahead], low[:ahead]), rows(q, q))
        return 0

    lax.fori_loop(0, PAIRS, grads, 0)
    gk_out[...] = (acc_k[: 2 * TILE, :TILE] + acc_k[: 2 * TILE, TILE:]) * (1.0 / LOG2E)
    send_gk.start()

    def results(pair, _):
        for t in range(TASKS):
            own = slice(2 * TILE, (3 + t) * TILE)
            ahead = (2 - t) * TILE
            q = qp[t, pair, :, : 2 * TILE]
            acc_k[own] += dot_nn(lanes(ds1[t, pair, ahead:], ds2[t, pair, ahead:]), rows(q, q))
            window = slice(t * TILE, (t + 3) * TILE)
            of_task = slice(t * TILE, (t + 1) * TILE)
            for mat, high, low, out, scale in (
                (vt, p1, p2, o_ref, None),
                (kt, ds1, ds2, dq_ref, SCORE_SCALE),
            ):
                m = mat[:, window]
                both = dot_nn(lanes(m, m), rows(high[t, pair], low[t, pair]))
                x = both[:TILE] + both[TILE:]
                if scale is not None:
                    x = x * scale
                for h in range(2):
                    columns = pl.ds(
                        pl.multiple_of(pair * 2 * TILE + h * TILE, TILE), TILE
                    )
                    out[of_task, columns] = x[:, h * TILE : (h + 1) * TILE].T
        return 0

    lax.fori_loop(0, PAIRS, results, 0)

    send_gv.wait_recv()
    dv_ref[...] = acc_v[2 * TILE :, :TILE] + acc_v[2 * TILE :, TILE:] + gv_in[...]
    send_gk.wait_recv()
    dk_ref[...] = (acc_k[2 * TILE :, :TILE] + acc_k[2 * TILE :, TILE:]) * (
        1.0 / LOG2E
    ) + gk_in[...]
    for copy in [*id_copies, send_k, send_v, send_id, send_gk, send_gv]:
        copy.wait_send()


def per_device(queries, keys, values, cotangent, doc_ids):
    tok_count = lax.axis_size("tok")
    head_count = lax.axis_size("head")
    vmem = pl.BlockSpec(memory_space=pltpu.VMEM)
    hbm = pl.BlockSpec(memory_space=pl.ANY)
    own = 2 * TILE
    win = 3 * TILE
    V = pltpu.VMEM
    return pl.pallas_call(
        functools.partial(kernel, tok_count, head_count),
        out_shape=(
            jax.ShapeDtypeStruct(queries.shape, f32),
            jax.ShapeDtypeStruct(queries.shape, f32),
            jax.ShapeDtypeStruct(keys.shape, f32),
            jax.ShapeDtypeStruct(keys.shape, f32),
        ),
        in_specs=[hbm, hbm, hbm, hbm, vmem],
        out_specs=(vmem, vmem, vmem, vmem),
        scratch_shapes=[
            V(queries.shape, f32),
            V(queries.shape, f32),
            *[V(keys.shape, f32) for _ in range(8)],
            V((8, TILE), f32),
            V((head_count, 8, TILE), f32),
            V((TASKS, 8, TILE), f32),
            V((TASKS, 8, TILE), f32),
            V((TASKS, win, TILE), f32),
            V((TASKS, PAIRS, own, 3 * TILE), bf16),
            V((TASKS, PAIRS, own, 2 * TILE), bf16),
            V((2 * own, 6 * TILE), bf16),
            V((2 * own, 4 * TILE), bf16),
            V((2 * TILE, 2 * own), bf16),
            V((2 * TILE, 2 * own), bf16),
            V((PAIRS, win, own), f32),
            V((PAIRS, win, own), f32),
            V((TASKS, PAIRS, win, own), f32),
            *[V((TASKS, PAIRS, win, own), bf16) for _ in range(4)],
            V((2 * own, 2 * TILE), f32),
            V((2 * own, 2 * TILE), f32),
            pltpu.SemaphoreType.DMA((4,)),
            pltpu.SemaphoreType.DMA((5,)),
            pltpu.SemaphoreType.DMA((5,)),
            pltpu.SemaphoreType.DMA((head_count - 1,)),
            pltpu.SemaphoreType.DMA((head_count - 1,)),
        ],
        compiler_params=pltpu.CompilerParams(
            collective_id=0, has_side_effects=True, vmem_limit_bytes=40 * 1024 * 1024
        ),
    )(queries, keys, values, cotangent, doc_ids.reshape(1, IDS))


def solution(mesh):
    placed = (
        P("tok", "head"),
        P("tok", "head"),
        P("tok", "head"),
        P("tok", "head"),
        P(("tok", "head")),
    )
    return jax.shard_map(
        per_device,
        mesh=mesh,
        in_specs=placed,
        out_specs=(P("tok", "head"), P("tok", "head"), P("tok", "head"), P("tok", "head")),
        check_vma=False,
    )
```

time: 110 us -> 44.4 us (0.40)
  the two profiles are of different devices: /device:TPU:120 before, /device:TPU:1 now
where the time goes in v1:
time: 44.4 us; the launch traced here: 44.1 us
  Pallas kernels  35.3 us (80%)
  local copies, waits for them, and re-layouts  8.16 us (18%)
  between operations  0.65 us (1%)
    pallas_call x1, Pallas kernels, per_device(): pl.pallas_call(functools.partial(kernel, tok_count, head_count), out_shap...  35.3 us
    unnamed x14, local copies, waits for them, and re-layouts  8.16 us

profile of v1, /device:TPU:1, one launch (start us, length us, event | category | flops | bytes accessed | tf_op | source)
XLA Modules:
  0.0 44.1 jit_solution(15317502083298262594)
XLA Ops:
  0.6 0.0 copy-start.4
  0.6 0.6 %copy-done.4 = s32[32]{0:T(128)S(1)} copy-done((s32[32]{0:T(128)S(1)}, s32[32]{0:T(128)}, u32[]{:S(2)}) %copy-start.4) | copy-done | bytes 152
  1.3 0.0 copy-start
  1.3 1.2 %copy-done = f32[256,1024]{1,0:T(8,128)S(1)} copy-done((f32[256,1024]{1,0:T(8,128)S(1)}, f32[256,1024]{1,0:T(8,128)}, u32[]{:S(2)}) %copy-start) | copy-done | bytes 1048600
  2.5 0.0 copy-start.1
  2.5 1.2 %copy-done.1 = f32[256,1024]{1,0:T(8,128)S(1)} copy-done((f32[256,1024]{1,0:T(8,128)S(1)}, f32[256,1024]{1,0:T(8,128)}, u32[]{:S(2)}) %copy-start.1) | copy-done | bytes 1048600
  3.7 0.0 copy-start.2
  3.7 0.9 %copy-done.2 = f32[256,128]{1,0:T(8,128)S(1)} copy-done((f32[256,128]{1,0:T(8,128)S(1)}, f32[256,128]{1,0:T(8,128)}, u32[]{:S(2)}) %copy-start.2) | copy-done | bytes 131096
  4.6 0.0 copy-start.3
  4.6 0.9 %copy-done.3 = f32[256,128]{1,0:T(8,128)S(1)} copy-done((f32[256,128]{1,0:T(8,128)S(1)}, f32[256,128]{1,0:T(8,128)}, u32[]{:S(2)}) %copy-start.3) | copy-done | bytes 131096
  5.5 35.3 %shard_map.84 = (f32[256,1024]{1,0:T(8,128)S(1)}, f32[256,1024]{1,0:T(8,128)S(1)}, f32[256,128]{1,0:T(8,128)S(1)}, f32[256,128]{1,0:T(8,128)S(1)}) custom-call(f32[256,1024]{1,0:T(8,128)S(1)} %copy-done, f32[256,128]{1,0:T(8,128)S(1)} %copy-done.2, f32[256,128]{1,0:T(8,128)S(1)} %copy-done.3, f32[256,1024]{1,0:T(8,128)S(1)} %copy-done.1, s32[1,32]{1,0:T(1,128)S(1)} %bitcast.1), custom_call_target="tpu_custom_call" | custom-call | tf_op jit(solution)/shard_map/pallas_call | solution.py:332
  40.9 1.0 %copy.13 = f32[256,1024]{1,0:T(8,128)} copy(f32[256,1024]{1,0:T(8,128)S(1)} %get-tuple-element.8) | data formatting | bytes 2097152
  41.9 1.0 %copy.14 = f32[256,1024]{1,0:T(8,128)} copy(f32[256,1024]{1,0:T(8,128)S(1)} %get-tuple-element.9) | data formatting | bytes 2097152
  42.8 0.7 %copy.15 = f32[256,128]{1,0:T(8,128)} copy(f32[256,128]{1,0:T(8,128)S(1)} %get-tuple-element.10) | data formatting | bytes 262144
  43.5 0.7 %copy.16 = f32[256,128]{1,0:T(8,128)} copy(f32[256,128]{1,0:T(8,128)S(1)} %get-tuple-element.11) | data formatting | bytes 262144
Async XLA Ops:
  0.6 0.7 %copy-start.4 = (s32[32]{0:T(128)S(1)}, s32[32]{0:T(128)}, u32[]{:S(2)}) copy-start(s32[32]{0:T(128)} %param.9) | copy-start | bytes 388
  1.3 1.2 %copy-start = (f32[256,1024]{1,0:T(8,128)S(1)}, f32[256,1024]{1,0:T(8,128)}, u32[]{:S(2)}) copy-start(f32[256,1024]{1,0:T(8,128)} %q_hbm.1) | copy-start | bytes 3145732
  2.5 1.2 %copy-start.1 = (f32[256,1024]{1,0:T(8,128)S(1)}, f32[256,1024]{1,0:T(8,128)}, u32[]{:S(2)}) copy-start(f32[256,1024]{1,0:T(8,128)} %g_hbm.1) | copy-start | bytes 3145732
  3.7 0.9 %copy-start.2 = (f32[256,128]{1,0:T(8,128)S(1)}, f32[256,128]{1,0:T(8,128)}, u32[]{:S(2)}) copy-start(f32[256,128]{1,0:T(8,128)} %k_hbm.1) | copy-start | bytes 393220
  4.6 0.9 %copy-start.3 = (f32[256,128]{1,0:T(8,128)S(1)}, f32[256,128]{1,0:T(8,128)}, u32[]{:S(2)}) copy-start(f32[256,128]{1,0:T(8,128)} %v_hbm.1) | copy-start | bytes 393220

commit v2 on v1

--- a/solution.py
+++ b/solution.py
@@ -59,7 +59,7 @@
     k_hbm,
     v_hbm,
     g_hbm,
-    ids_ref,
+    ids_hbm,
     o_ref,
     dq_ref,
     dk_ref,
@@ -74,6 +74,7 @@
     gv_out,
     gk_in,
     gv_in,
+    id_raw,
     id_mine,
     id_got,
     id_own,
@@ -109,7 +110,7 @@
     loads = [
         pltpu.make_async_copy(src, dst, local_sem.at[i])
         for i, (src, dst) in enumerate(
-            [(k_hbm, k_own), (v_hbm, v_own), (q_hbm, qf), (g_hbm, gf)]
+            [(ids_hbm, id_raw), (k_hbm, k_own), (v_hbm, v_own), (q_hbm, qf), (g_hbm, gf)]
         )
     ]
     for load in loads:
@@ -123,7 +124,8 @@
         lax.broadcasted_iota(jnp.int32, (IDS, TILE), 1) % IDS
         == lax.broadcasted_iota(jnp.int32, (IDS, TILE), 0)
     )
-    ids = jnp.broadcast_to(ids_ref[...].astype(f32), (8, IDS)).astype(bf16)
+    loads[0].wait()
+    ids = jnp.broadcast_to(id_raw[...].astype(f32), (8, IDS)).astype(bf16)
     id_mine[...] = dot_nn(ids, jnp.where(spread, 1.0, 0.0).astype(bf16))
     id_got[head] = id_mine[...]
 
@@ -170,12 +172,12 @@
         vc[base : base + 2 * TILE] = lanes(a, a, b, b)
         vt[:, base : base + 2 * TILE] = rows(*parts2(v.T))
 
-    loads[0].wait()
     loads[1].wait()
+    loads[2].wait()
     pack_k(k_own[...], 2 * TILE)
     pack_v(v_own[...], 2 * TILE)
-    loads[2].wait()
     loads[3].wait()
+    loads[4].wait()
 
     def q_pack(t, pair):
         a, b, c = (qp[t, pair, :, i * TILE : (i + 1) * TILE] for i in range(3))
@@ -199,7 +201,7 @@
             dp_own[pair, kept] = dot_nt(vc[own], g_pack(t, pair))
         return 0
 
-    lax.fori_loop(0, PAIRS, own_scores, 0)
+    lax.fori_loop(0, PAIRS, own_scores, 0, unroll=True)
 
     for copy in id_copies:
         copy.wait_recv()
@@ -249,7 +251,7 @@
             acc_v[before] += dot_nn(lanes(high[:ahead], low[:ahead]), rows(g, g))
         return 0
 
-    lax.fori_loop(0, PAIRS, probs, 0)
+    lax.fori_loop(0, PAIRS, probs, 0, unroll=True)
     gv_out[...] = acc_v[: 2 * TILE, :TILE] + acc_v[: 2 * TILE, TILE:]
     send_gv.start()
 
@@ -261,7 +263,7 @@
             acc_v[own] += dot_nn(lanes(p1[t, pair, ahead:], p2[t, pair, ahead:]), rows(g, g))
         return 0
 
-    lax.fori_loop(0, PAIRS, own_values, 0)
+    lax.fori_loop(0, PAIRS, own_values, 0, unroll=True)
 
     send_v.wait_recv()
     pack_v(v_prev[...], 0)
@@ -281,7 +283,7 @@
             acc_k[before] += dot_nn(lanes(high[:ahead], low[:ahead]), rows(q, q))
         return 0
 
-    lax.fori_loop(0, PAIRS, grads, 0)
+    lax.fori_loop(0, PAIRS, grads, 0, unroll=True)
     gk_out[...] = (acc_k[: 2 * TILE, :TILE] + acc_k[: 2 * TILE, TILE:]) * (1.0 / LOG2E)
     send_gk.start()
 
@@ -309,7 +311,7 @@
                     out[of_task, columns] = x[:, h * TILE : (h + 1) * TILE].T
         return 0
 
-    lax.fori_loop(0, PAIRS, results, 0)
+    lax.fori_loop(0, PAIRS, results, 0, unroll=True)
 
     send_gv.wait_recv()
     dv_ref[...] = acc_v[2 * TILE :, :TILE] + acc_v[2 * TILE :, TILE:] + gv_in[...]
@@ -321,6 +323,17 @@
         copy.wait_send()
 
 
+def place(a, b, c, d, a_out, b_out, c_out, d_out, sem):
+    copies = [
+        pltpu.make_async_copy(src, dst, sem.at[i])
+        for i, (src, dst) in enumerate([(a, a_out), (b, b_out), (c, c_out), (d, d_out)])
+    ]
+    for copy in copies:
+        copy.start()
+    for copy in copies:
+        copy.wait()
+
+
 def per_device(queries, keys, values, cotangent, doc_ids):
     tok_count = lax.axis_size("tok")
     head_count = lax.axis_size("head")
@@ -329,7 +342,7 @@
     own = 2 * TILE
     win = 3 * TILE
     V = pltpu.VMEM
-    return pl.pallas_call(
+    found = pl.pallas_call(
         functools.partial(kernel, tok_count, head_count),
         out_shape=(
             jax.ShapeDtypeStruct(queries.shape, f32),
@@ -337,12 +350,13 @@
             jax.ShapeDtypeStruct(keys.shape, f32),
             jax.ShapeDtypeStruct(keys.shape, f32),
         ),
-        in_specs=[hbm, hbm, hbm, hbm, vmem],
+        in_specs=[hbm] * 5,
         out_specs=(vmem, vmem, vmem, vmem),
         scratch_shapes=[
             V(queries.shape, f32),
             V(queries.shape, f32),
             *[V(keys.shape, f32) for _ in range(8)],
+            V((1, IDS), jnp.int32),
             V((8, TILE), f32),
             V((head_count, 8, TILE), f32),
             V((TASKS, 8, TILE), f32),
@@ -360,7 +374,7 @@
             *[V((TASKS, PAIRS, win, own), bf16) for _ in range(4)],
             V((2 * own, 2 * TILE), f32),
             V((2 * own, 2 * TILE), f32),
-            pltpu.SemaphoreType.DMA((4,)),
+            pltpu.SemaphoreType.DMA((5,)),
             pltpu.SemaphoreType.DMA((5,)),
             pltpu.SemaphoreType.DMA((5,)),
             pltpu.SemaphoreType.DMA((head_count - 1,)),
@@ -369,7 +383,20 @@
         compiler_params=pltpu.CompilerParams(
             collective_id=0, has_side_effects=True, vmem_limit_bytes=40 * 1024 * 1024
         ),
-    )(queries, keys, values, cotangent, doc_ids.reshape(1, IDS))
+    )(
+        *(
+            pltpu.with_memory_space_constraint(x, pltpu.HBM)
+            for x in (queries, keys, values, cotangent, doc_ids.reshape(1, IDS))
+        )
+    )
+    return pl.pallas_call(
+        place,
+        out_shape=tuple(jax.ShapeDtypeStruct(x.shape, f32) for x in found),
+        in_specs=[hbm] * 4,
+        out_specs=(hbm,) * 4,
+        scratch_shapes=[pltpu.SemaphoreType.DMA((4,))],
+        compiler_params=pltpu.CompilerParams(vmem_limit_bytes=1024 * 1024),
+    )(*found)
 
 
 def solution(mesh):

time: 44.4 us -> 33.5 us (0.75)
  local copies, waits for them, and re-layouts: 8.16 us -> 0 us
  Pallas kernels: 35.3 us -> 32.7 us
    unnamed x14 -> x0, local copies, waits for them, and re-layouts: 8.16 us -> none
    pallas_call x1, Pallas kernels: 35.3 us -> 31.3 us  [per_device(): pl.pallas_call(functools.partial(kernel, tok_count, head_count), out_shap...]
    pallas_call x0 -> x1, Pallas kernels: none -> 1.43 us  [per_device(): pl.pallas_call(place, out_shape=tuple((jax.ShapeDtypeStruct(x.shape, f32)...]
where the time goes in v2:
time: 33.5 us; the launch traced here: 33.3 us
  Pallas kernels  32.7 us (98%)
  between operations  0.64 us (2%)
    pallas_call x1, Pallas kernels, per_device(): pl.pallas_call(functools.partial(kernel, tok_count, head_count), out_shap...  31.3 us
    pallas_call x1, Pallas kernels, per_device(): pl.pallas_call(place, out_shape=tuple((jax.ShapeDtypeStruct(x.shape, f32)...  1.43 us

profile of v2, /device:TPU:1, one launch (start us, length us, event | category | flops | bytes accessed | tf_op | source)
XLA Modules:
  0.0 33.3 jit_solution(15415697922077120794)
XLA Ops:
  0.6 31.3 %shard_map.84 = (f32[256,1024]{1,0:T(8,128)S(1)}, f32[256,1024]{1,0:T(8,128)S(1)}, f32[256,128]{1,0:T(8,128)S(1)}, f32[256,128]{1,0:T(8,128)S(1)}) custom-call(f32[256,1024]{1,0:T(8,128)} %q_hbm.1, f32[256,128]{1,0:T(8,128)} %k_hbm.1, f32[256,128]{1,0:T(8,128)} %v_hbm.1, f32[256,1024]{1,0:T(8,128)} %g_hbm.1, s32[1,32]{1,0:T(1,128)} %bitcast.1), custom_call_target="tpu_custom_call" | custom-call | tf_op jit(solution)/shard_map/pallas_call | solution.py:345
  31.9 1.4 %shard_map.85 = (f32[256,1024]{1,0:T(8,128)}, f32[256,1024]{1,0:T(8,128)}, f32[256,128]{1,0:T(8,128)}, f32[256,128]{1,0:T(8,128)}) custom-call(f32[256,1024]{1,0:T(8,128)S(1)} %get-tuple-element.8.a, f32[256,1024]{1,0:T(8,128)S(1)} %get-tuple-element.9.b, f32[256,128]{1,0:T(8,128)S(1)} %get-tuple-element.10.c, f32[256,128]{1,0:T(8,128)S(1)} %get-tuple-element.11.d), custom_call_target="tpu_custom_call" | custom-call | tf_op jit(solution)/shard_map/pallas_call | solution.py:392

commit v3 on v2

--- a/solution.py
+++ b/solution.py
@@ -116,9 +116,29 @@
     for load in loads:
         load.start()
 
+    has_prev = tok > 0
+    has_next = tok < tok_count - 1
+
     barrier = pltpu.get_barrier_semaphore()
-    for device in [nxt, prv, *peers]:
+
+    def greet(device):
         pl.semaphore_signal(barrier, inc=1, device_id=device, device_id_type=MESH)
+
+    pl.when(has_next)(lambda: greet(nxt))
+    pl.when(has_prev)(lambda: greet(prv))
+    for device in peers:
+        greet(device)
+
+    @pl.when(jnp.logical_not(has_prev))
+    def _():
+        k_prev[...] = jnp.zeros_like(k_prev)
+        v_prev[...] = jnp.zeros_like(v_prev)
+        id_prev[...] = jnp.full_like(id_prev, -1.0)
+
+    @pl.when(jnp.logical_not(has_next))
+    def _():
+        gk_in[...] = jnp.zeros_like(gk_in)
+        gv_in[...] = jnp.zeros_like(gv_in)
 
     spread = (
         lax.broadcasted_iota(jnp.int32, (IDS, TILE), 1) % IDS
@@ -129,7 +149,9 @@
     id_mine[...] = dot_nn(ids, jnp.where(spread, 1.0, 0.0).astype(bf16))
     id_got[head] = id_mine[...]
 
-    pl.semaphore_wait(barrier, head_count + 1)
+    pl.semaphore_wait(
+        barrier, head_count - 1 + has_prev.astype(jnp.int32) + has_next.astype(jnp.int32)
+    )
 
     id_copies = [
         pltpu.make_async_remote_copy(
@@ -160,7 +182,7 @@
     send_id = to(nxt, 2, id_own, id_prev)
     send_gk = to(prv, 3, gk_out, gk_in)
     send_gv = to(prv, 4, gv_out, gv_in)
-    send_k.start()
+    pl.when(has_next)(send_k.start)
 
     def pack_k(k, base):
         a, b, c = parts3(k)
@@ -211,11 +233,10 @@
         for j in range(1, TILE // IDS):
             row = jnp.where(lane_group == j, id_got[4 * t + j], row)
         id_own[t] = row
-    send_id.start()
-    send_v.start()
-
-    send_id.wait_recv()
-    id_rows = [jnp.where(tok == 0, -1.0, id_prev[t]) for t in range(TASKS)]
+    pl.when(has_next)(send_id.start)
+    pl.when(has_next)(send_v.start)
+    pl.when(has_prev)(send_id.wait_recv)
+    id_rows = [id_prev[t] for t in range(TASKS)]
     id_rows += [id_own[t] for t in range(TASKS)]
     wide = [jnp.broadcast_to(r[0:1], (TILE, TILE)) for r in id_rows]
     causal = lax.broadcasted_iota(jnp.int32, (TILE, TILE), 0) <= lax.broadcasted_iota(
@@ -228,7 +249,7 @@
                 allowed = allowed & causal
             bias[t, j * TILE : (j + 1) * TILE] = jnp.where(allowed, 0.0, NEG)
 
-    send_k.wait_recv()
+    pl.when(has_prev)(send_k.wait_recv)
     pack_k(k_prev[...], 0)
 
     acc_k[...] = jnp.zeros_like(acc_k)
@@ -253,7 +274,7 @@
 
     lax.fori_loop(0, PAIRS, probs, 0, unroll=True)
     gv_out[...] = acc_v[: 2 * TILE, :TILE] + acc_v[: 2 * TILE, TILE:]
-    send_gv.start()
+    pl.when(has_prev)(send_gv.start)
 
     def own_values(pair, _):
         for t in range(TASKS):
@@ -265,7 +286,7 @@
 
     lax.fori_loop(0, PAIRS, own_values, 0, unroll=True)
 
-    send_v.wait_recv()
+    pl.when(has_prev)(send_v.wait_recv)
     pack_v(v_prev[...], 0)
 
     def grads(pair, _):
@@ -285,7 +306,7 @@
 
     lax.fori_loop(0, PAIRS, grads, 0, unroll=True)
     gk_out[...] = (acc_k[: 2 * TILE, :TILE] + acc_k[: 2 * TILE, TILE:]) * (1.0 / LOG2E)
-    send_gk.start()
+    pl.when(has_prev)(send_gk.start)
 
     def results(pair, _):
         for t in range(TASKS):
@@ -313,14 +334,18 @@
 
     lax.fori_loop(0, PAIRS, results, 0, unroll=True)
 
-    send_gv.wait_recv()
+    pl.when(has_next)(send_gv.wait_recv)
     dv_ref[...] = acc_v[2 * TILE :, :TILE] + acc_v[2 * TILE :, TILE:] + gv_in[...]
-    send_gk.wait_recv()
+    pl.when(has_next)(send_gk.wait_recv)
     dk_ref[...] = (acc_k[2 * TILE :, :TILE] + acc_k[2 * TILE :, TILE:]) * (
         1.0 / LOG2E
     ) + gk_in[...]
-    for copy in [*id_copies, send_k, send_v, send_id, send_gk, send_gv]:
+    for copy in id_copies:
         copy.wait_send()
+    for copy in (send_k, send_v, send_id):
+        pl.when(has_next)(copy.wait_send)
+    for copy in (send_gk, send_gv):
+        pl.when(has_prev)(copy.wait_send)
 
 
 def place(a, b, c, d, a_out, b_out, c_out, d_out, sem):

time: 33.5 us -> 27 us (0.81)
  the two profiles are of different devices: /device:TPU:1 before, /device:TPU:120 now
where the time goes in v3:
time: 27 us; the launch traced here: 26.9 us
  Pallas kernels  26.2 us (97%)
  between operations  0.64 us (2%)
    pallas_call x1, Pallas kernels, per_device(): pl.pallas_call(functools.partial(kernel, tok_count, head_count), out_shap...  24.8 us
    pallas_call x1, Pallas kernels, per_device(): pl.pallas_call(place, out_shape=tuple((jax.ShapeDtypeStruct(x.shape, f32)...  1.43 us

profile of v3, /device:TPU:120, one launch (start us, length us, event | category | flops | bytes accessed | tf_op | source)
XLA Modules:
  0.0 26.9 jit_solution(1103983481079799699)
XLA Ops:
  0.6 24.8 %shard_map.84 = (f32[256,1024]{1,0:T(8,128)S(1)}, f32[256,1024]{1,0:T(8,128)S(1)}, f32[256,128]{1,0:T(8,128)S(1)}, f32[256,128]{1,0:T(8,128)S(1)}) custom-call(f32[256,1024]{1,0:T(8,128)} %q_hbm.1, f32[256,128]{1,0:T(8,128)} %k_hbm.1, f32[256,128]{1,0:T(8,128)} %v_hbm.1, f32[256,1024]{1,0:T(8,128)} %g_hbm.1, s32[1,32]{1,0:T(1,128)} %bitcast.1), custom_call_target="tpu_custom_call" | custom-call | tf_op jit(solution)/shard_map/pallas_call | solution.py:370
  25.4 1.4 %shard_map.85 = (f32[256,1024]{1,0:T(8,128)}, f32[256,1024]{1,0:T(8,128)}, f32[256,128]{1,0:T(8,128)}, f32[256,128]{1,0:T(8,128)}) custom-call(f32[256,1024]{1,0:T(8,128)S(1)} %get-tuple-element.8.a, f32[256,1024]{1,0:T(8,128)S(1)} %get-tuple-element.9.b, f32[256,128]{1,0:T(8,128)S(1)} %get-tuple-element.10.c, f32[256,128]{1,0:T(8,128)S(1)} %get-tuple-element.11.d), custom_call_target="tpu_custom_call" | custom-call | tf_op jit(solution)/shard_map/pallas_call | solution.py:417

commit v4 on v3

--- a/solution.py
+++ b/solution.py
@@ -77,8 +77,6 @@
     id_raw,
     id_mine,
     id_got,
-    id_own,
-    id_prev,
     bias,
     qp,
     gp,
@@ -88,6 +86,8 @@
     vt,
     s_own,
     dp_own,
+    inverse,
+    delta,
     pf,
     p1,
     p2,
@@ -100,12 +100,34 @@
     recv_sem,
     id_send_sem,
     id_recv_sem,
+    ready_sem,
 ):
     tok = lax.axis_index("tok")
     head = lax.axis_index("head")
     nxt = (lax.rem(tok + 1, tok_count), head)
     prv = (lax.rem(tok + tok_count - 1, tok_count), head)
-    peers = [(tok, lax.rem(head + j, head_count)) for j in range(1, head_count)]
+    has_prev = tok > 0
+    has_next = tok < tok_count - 1
+
+    def rank(h):
+        return h + jnp.where((tok == 0) & (h == 0), head_count, 0)
+
+    others = [lax.rem(head + j, head_count) for j in range(1, head_count)]
+    mine = rank(head)
+    above = [rank(h) > mine for h in others]
+
+    def total(flags):
+        return sum(flag.astype(jnp.int32) for flag in flags)
+
+    barrier = pltpu.get_barrier_semaphore()
+
+    def signal(semaphore, device):
+        pl.semaphore_signal(semaphore, inc=1, device_id=device, device_id_type=MESH)
+
+    pl.when(has_next)(lambda: signal(barrier, nxt))
+    pl.when(has_prev)(lambda: signal(barrier, prv))
+    for h, flag in zip(others, above):
+        pl.when(flag)(functools.partial(signal, barrier, (tok, h)))
 
     loads = [
         pltpu.make_async_copy(src, dst, local_sem.at[i])
@@ -116,24 +138,12 @@
     for load in loads:
         load.start()
 
-    has_prev = tok > 0
-    has_next = tok < tok_count - 1
-
-    barrier = pltpu.get_barrier_semaphore()
-
-    def greet(device):
-        pl.semaphore_signal(barrier, inc=1, device_id=device, device_id_type=MESH)
-
-    pl.when(has_next)(lambda: greet(nxt))
-    pl.when(has_prev)(lambda: greet(prv))
-    for device in peers:
-        greet(device)
-
     @pl.when(jnp.logical_not(has_prev))
     def _():
         k_prev[...] = jnp.zeros_like(k_prev)
         v_prev[...] = jnp.zeros_like(v_prev)
-        id_prev[...] = jnp.full_like(id_prev, -1.0)
+        for h in range(head_count):
+            id_got[head_count + h] = jnp.full_like(id_mine, -1.0)
 
     @pl.when(jnp.logical_not(has_next))
     def _():
@@ -149,23 +159,24 @@
     id_mine[...] = dot_nn(ids, jnp.where(spread, 1.0, 0.0).astype(bf16))
     id_got[head] = id_mine[...]
 
-    pl.semaphore_wait(
-        barrier, head_count - 1 + has_prev.astype(jnp.int32) + has_next.astype(jnp.int32)
-    )
-
-    id_copies = [
-        pltpu.make_async_remote_copy(
-            src_ref=id_mine,
-            dst_ref=id_got.at[head],
-            send_sem=id_send_sem.at[j],
-            recv_sem=id_recv_sem.at[j],
+    pl.semaphore_wait(barrier, head_count - 1 - total(above) + total([has_next, has_prev]))
+
+    def send_ids(device, i, src, slot):
+        return pltpu.make_async_remote_copy(
+            src_ref=src,
+            dst_ref=id_got.at[slot],
+            send_sem=id_send_sem.at[i],
+            recv_sem=id_recv_sem.at[i],
             device_id=device,
             device_id_type=MESH,
         )
-        for j, device in enumerate(peers)
+
+    slot = head_count + head
+    ids_next = send_ids(nxt, 0, id_mine, slot)
+    ids_beside = [send_ids((tok, h), 1 + j, id_mine, head) for j, h in enumerate(others)]
+    ids_on = [
+        send_ids((tok, h), head_count + j, id_got.at[slot], slot) for j, h in enumerate(others)
     ]
-    for copy in id_copies:
-        copy.start()
 
     def to(device, i, src, dst):
         return pltpu.make_async_remote_copy(
@@ -179,10 +190,22 @@
 
     send_k = to(nxt, 0, k_hbm, k_prev)
     send_v = to(nxt, 1, v_hbm, v_prev)
-    send_id = to(nxt, 2, id_own, id_prev)
-    send_gk = to(prv, 3, gk_out, gk_in)
-    send_gv = to(prv, 4, gv_out, gv_in)
-    pl.when(has_next)(send_k.start)
+    halves = [pl.ds(t * TILE, TILE) for t in range(TASKS)]
+    send_gv = [to(prv, 2 + t, gv_out.at[r], gv_in.at[r]) for t, r in enumerate(halves)]
+    send_gk = [to(prv, 4 + t, gk_out.at[r], gk_in.at[r]) for t, r in enumerate(halves)]
+
+    @pl.when(has_next)
+    def _():
+        ids_next.start()
+        send_k.start()
+        send_v.start()
+
+    for h, copy, flag in zip(others, ids_beside, above):
+
+        @pl.when(jnp.logical_not(flag))
+        def _():
+            signal(ready_sem, (tok, h))
+            copy.start()
 
     def pack_k(k, base):
         a, b, c = parts3(k)
@@ -200,6 +223,15 @@
     pack_v(v_own[...], 2 * TILE)
     loads[3].wait()
     loads[4].wait()
+
+    waiting = total(above)
+
+    @pl.when(waiting > 0)
+    def _():
+        pl.semaphore_wait(ready_sem, waiting)
+
+    for copy, flag in zip(ids_beside, above):
+        pl.when(flag)(copy.start)
 
     def q_pack(t, pair):
         a, b, c = (qp[t, pair, :, i * TILE : (i + 1) * TILE] for i in range(3))
@@ -225,20 +257,43 @@
 
     lax.fori_loop(0, PAIRS, own_scores, 0, unroll=True)
 
-    for copy in id_copies:
+    @pl.when(has_prev)
+    def _():
+        ids_next.wait_recv()
+        for copy in ids_on:
+            copy.start()
+
+
+    pl.when(has_prev)(send_k.wait_recv)
+    pack_k(k_prev[...], 0)
+
+    acc_k[...] = jnp.zeros_like(acc_k)
+    acc_v[...] = jnp.zeros_like(acc_v)
+
+    def earlier_scores(pair, _):
+        for t in range(TASKS):
+            before = slice(t * TILE, 2 * TILE)
+            pf[t, pair, : (2 - t) * TILE] = dot_nt(kc[before], q_pack(t, pair))
+        return 0
+
+    lax.fori_loop(0, PAIRS, earlier_scores, 0, unroll=True)
+
+    for copy in ids_beside:
         copy.wait_recv()
+
+    @pl.when(has_prev)
+    def _():
+        for copy in ids_on:
+            copy.wait_recv()
+
     lane_group = lax.broadcasted_iota(jnp.int32, (8, TILE), 1) // IDS
-    for t in range(TASKS):
-        row = id_got[4 * t]
-        for j in range(1, TILE // IDS):
-            row = jnp.where(lane_group == j, id_got[4 * t + j], row)
-        id_own[t] = row
-    pl.when(has_next)(send_id.start)
-    pl.when(has_next)(send_v.start)
-    pl.when(has_prev)(send_id.wait_recv)
-    id_rows = [id_prev[t] for t in range(TASKS)]
-    id_rows += [id_own[t] for t in range(TASKS)]
-    wide = [jnp.broadcast_to(r[0:1], (TILE, TILE)) for r in id_rows]
+    per_tile = TILE // IDS
+    wide = []
+    for first in (head_count, head_count + per_tile, 0, per_tile):
+        row = id_got[first]
+        for j in range(1, per_tile):
+            row = jnp.where(lane_group == j, id_got[first + j], row)
+        wide.append(jnp.broadcast_to(row[0:1], (TILE, TILE)))
     causal = lax.broadcasted_iota(jnp.int32, (TILE, TILE), 0) <= lax.broadcasted_iota(
         jnp.int32, (TILE, TILE), 1
     )
@@ -249,79 +304,86 @@
                 allowed = allowed & causal
             bias[t, j * TILE : (j + 1) * TILE] = jnp.where(allowed, 0.0, NEG)
 
-    pl.when(has_prev)(send_k.wait_recv)
-    pack_k(k_prev[...], 0)
-
-    acc_k[...] = jnp.zeros_like(acc_k)
-    acc_v[...] = jnp.zeros_like(acc_v)
-
-    def probs(pair, _):
-        for t in range(TASKS):
-            before = slice(t * TILE, 2 * TILE)
-            kept = slice(t * TILE, (1 + 2 * t) * TILE)
-            b = bias[t]
-            s = rows(dot_nt(kc[before], q_pack(t, pair)), s_own[pair, kept]) + lanes(b, b)
-            weights = jnp.exp2(s - jnp.max(s, axis=0, keepdims=True))
-            p = weights * (1.0 / jnp.sum(weights, axis=0, keepdims=True))
-            pf[t, pair] = p
-            high, low = parts2(p)
-            p1[t, pair] = high
-            p2[t, pair] = low
-            g = gp[t, pair]
-            ahead = (2 - t) * TILE
-            acc_v[before] += dot_nn(lanes(high[:ahead], low[:ahead]), rows(g, g))
+    def probs(t, pair, _):
+        before = slice(t * TILE, 2 * TILE)
+        kept = slice(t * TILE, (1 + 2 * t) * TILE)
+        ahead = (2 - t) * TILE
+        b = bias[t]
+        s_prev = pf[t, pair, :ahead] + lanes(b[:ahead], b[:ahead])
+        s_here = s_own[pair, kept] + lanes(b[ahead:], b[ahead:])
+        top = jnp.maximum(
+            jnp.max(s_prev, axis=0, keepdims=True), jnp.max(s_here, axis=0, keepdims=True)
+        )
+        w_prev = jnp.exp2(s_prev - top)
+        w_here = jnp.exp2(s_here - top)
+        s_own[pair, kept] = w_here
+        inv = 1.0 / (
+            jnp.sum(w_prev, axis=0, keepdims=True) + jnp.sum(w_here, axis=0, keepdims=True)
+        )
+        inverse[t, pair] = inv
+        p = w_prev * inv
+        pf[t, pair, :ahead] = p
+        high, low = parts2(p)
+        p1[t, pair, :ahead] = high
+        p2[t, pair, :ahead] = low
+        g = gp[t, pair]
+        acc_v[before] += dot_nn(lanes(high, low), rows(g, g))
         return 0
 
-    lax.fori_loop(0, PAIRS, probs, 0, unroll=True)
-    gv_out[...] = acc_v[: 2 * TILE, :TILE] + acc_v[: 2 * TILE, TILE:]
-    pl.when(has_prev)(send_gv.start)
-
-    def own_values(pair, _):
-        for t in range(TASKS):
-            own = slice(2 * TILE, (3 + t) * TILE)
-            ahead = (2 - t) * TILE
-            g = gp[t, pair]
-            acc_v[own] += dot_nn(lanes(p1[t, pair, ahead:], p2[t, pair, ahead:]), rows(g, g))
-        return 0
-
-    lax.fori_loop(0, PAIRS, own_values, 0, unroll=True)
+    for t in range(TASKS):
+        lax.fori_loop(0, PAIRS, functools.partial(probs, t), 0, unroll=True)
+        tile = slice(t * TILE, (t + 1) * TILE)
+        gv_out[tile] = acc_v[tile, :TILE] + acc_v[tile, TILE:]
+        pl.when(has_prev)(send_gv[t].start)
 
     pl.when(has_prev)(send_v.wait_recv)
     pack_v(v_prev[...], 0)
 
-    def grads(pair, _):
-        for t in range(TASKS):
-            before = slice(t * TILE, 2 * TILE)
-            kept = slice(t * TILE, (1 + 2 * t) * TILE)
-            dp = rows(dot_nt(vc[before], g_pack(t, pair)), dp_own[pair, kept])
-            p = pf[t, pair]
-            delta = jnp.sum(p * dp, axis=0, keepdims=True)
-            high, low = parts2(p * (dp - delta))
-            ds1[t, pair] = high
-            ds2[t, pair] = low
-            q = qp[t, pair, :, : 2 * TILE]
-            ahead = (2 - t) * TILE
-            acc_k[before] += dot_nn(lanes(high[:ahead], low[:ahead]), rows(q, q))
+    def grads(t, pair, _):
+        before = slice(t * TILE, 2 * TILE)
+        kept = slice(t * TILE, (1 + 2 * t) * TILE)
+        ahead = (2 - t) * TILE
+        of_own = jnp.sum(s_own[pair, kept] * dp_own[pair, kept], axis=0, keepdims=True)
+        dp = dot_nt(vc[before], g_pack(t, pair))
+        p = pf[t, pair, :ahead]
+        row_delta = of_own * inverse[t, pair] + jnp.sum(p * dp, axis=0, keepdims=True)
+        delta[t, pair] = row_delta
+        high, low = parts2(p * (dp - row_delta))
+        ds1[t, pair, :ahead] = high
+        ds2[t, pair, :ahead] = low
+        q = qp[t, pair, :, : 2 * TILE]
+        acc_k[before] += dot_nn(lanes(high, low), rows(q, q))
         return 0
 
-    lax.fori_loop(0, PAIRS, grads, 0, unroll=True)
-    gk_out[...] = (acc_k[: 2 * TILE, :TILE] + acc_k[: 2 * TILE, TILE:]) * (1.0 / LOG2E)
-    pl.when(has_prev)(send_gk.start)
+    for t in range(TASKS):
+        lax.fori_loop(0, PAIRS, functools.partial(grads, t), 0, unroll=True)
+        tile = slice(t * TILE, (t + 1) * TILE)
+        gk_out[tile] = (acc_k[tile, :TILE] + acc_k[tile, TILE:]) * (1.0 / LOG2E)
+        pl.when(has_prev)(send_gk[t].start)
 
     def results(pair, _):
         for t in range(TASKS):
             own = slice(2 * TILE, (3 + t) * TILE)
+            kept = slice(t * TILE, (1 + 2 * t) * TILE)
             ahead = (2 - t) * TILE
+            p = s_own[pair, kept] * inverse[t, pair]
+            p_high, p_low = parts2(p)
+            d_high, d_low = parts2(p * (dp_own[pair, kept] - delta[t, pair]))
+            g = gp[t, pair]
+            acc_v[own] += dot_nn(lanes(p_high, p_low), rows(g, g))
             q = qp[t, pair, :, : 2 * TILE]
-            acc_k[own] += dot_nn(lanes(ds1[t, pair, ahead:], ds2[t, pair, ahead:]), rows(q, q))
+            acc_k[own] += dot_nn(lanes(d_high, d_low), rows(q, q))
             window = slice(t * TILE, (t + 3) * TILE)
             of_task = slice(t * TILE, (t + 1) * TILE)
-            for mat, high, low, out, scale in (
-                (vt, p1, p2, o_ref, None),
-                (kt, ds1, ds2, dq_ref, SCORE_SCALE),
+            for mat, first, second, high, low, out, scale in (
+                (vt, p1, p2, p_high, p_low, o_ref, None),
+                (kt, ds1, ds2, d_high, d_low, dq_ref, SCORE_SCALE),
             ):
                 m = mat[:, window]
-                both = dot_nn(lanes(m, m), rows(high[t, pair], low[t, pair]))
+                both = dot_nn(
+                    lanes(m, m),
+                    rows(first[t, pair, :ahead], high, second[t, pair, :ahead], low),
+                )
                 x = both[:TILE] + both[TILE:]
                 if scale is not None:
                     x = x * scale
@@ -334,17 +396,18 @@
 
     lax.fori_loop(0, PAIRS, results, 0, unroll=True)
 
-    pl.when(has_next)(send_gv.wait_recv)
-    dv_ref[...] = acc_v[2 * TILE :, :TILE] + acc_v[2 * TILE :, TILE:] + gv_in[...]
-    pl.when(has_next)(send_gk.wait_recv)
-    dk_ref[...] = (acc_k[2 * TILE :, :TILE] + acc_k[2 * TILE :, TILE:]) * (
-        1.0 / LOG2E
-    ) + gk_in[...]
-    for copy in id_copies:
+    dv_own = acc_v[2 * TILE :, :TILE] + acc_v[2 * TILE :, TILE:]
+    dk_own = (acc_k[2 * TILE :, :TILE] + acc_k[2 * TILE :, TILE:]) * (1.0 / LOG2E)
+    for own, sent, got, out in ((dv_own, send_gv, gv_in, dv_ref), (dk_own, send_gk, gk_in, dk_ref)):
+        for t in range(TASKS):
+            tile = slice(t * TILE, (t + 1) * TILE)
+            pl.when(has_next)(sent[t].wait_recv)
+            out[tile] = own[tile] + got[tile]
+    for copy in ids_beside:
         copy.wait_send()
-    for copy in (send_k, send_v, send_id):
+    for copy in (ids_next, send_k, send_v):
         pl.when(has_next)(copy.wait_send)
-    for copy in (send_gk, send_gv):
+    for copy in (*ids_on, *send_gk, *send_gv):
         pl.when(has_prev)(copy.wait_send)
 
 
@@ -383,9 +446,7 @@
             *[V(keys.shape, f32) for _ in range(8)],
             V((1, IDS), jnp.int32),
             V((8, TILE), f32),
-            V((head_count, 8, TILE), f32),
-            V((TASKS, 8, TILE), f32),
-            V((TASKS, 8, TILE), f32),
+            V((2 * head_count, 8, TILE), f32),
             V((TASKS, win, TILE), f32),
             V((TASKS, PAIRS, own, 3 * TILE), bf16),
             V((TASKS, PAIRS, own, 2 * TILE), bf16),
@@ -395,15 +456,18 @@
             V((2 * TILE, 2 * own), bf16),
             V((PAIRS, win, own), f32),
             V((PAIRS, win, own), f32),
-            V((TASKS, PAIRS, win, own), f32),
-            *[V((TASKS, PAIRS, win, own), bf16) for _ in range(4)],
+            V((TASKS, PAIRS, 1, own), f32),
+            V((TASKS, PAIRS, 1, own), f32),
+            V((TASKS, PAIRS, own, own), f32),
+            *[V((TASKS, PAIRS, own, own), bf16) for _ in range(4)],
             V((2 * own, 2 * TILE), f32),
             V((2 * own, 2 * TILE), f32),
             pltpu.SemaphoreType.DMA((5,)),
-            pltpu.SemaphoreType.DMA((5,)),
-            pltpu.SemaphoreType.DMA((5,)),
-            pltpu.SemaphoreType.DMA((head_count - 1,)),
-            pltpu.SemaphoreType.DMA((head_count - 1,)),
+            pltpu.SemaphoreType.DMA((6,)),
+            pltpu.SemaphoreType.DMA((6,)),
+            pltpu.SemaphoreType.DMA((2 * head_count,)),
+            pltpu.SemaphoreType.DMA((2 * head_count,)),
+            pltpu.SemaphoreType.REGULAR,
         ],
         compiler_params=pltpu.CompilerParams(
             collective_id=0, has_side_effects=True, vmem_limit_bytes=40 * 1024 * 1024

time: 27 us -> 25.6 us (0.948)
  Pallas kernels: 26.2 us -> 24.8 us
    pallas_call x1, Pallas kernels: 24.8 us -> 23.4 us  [per_device(): pl.pallas_call(functools.partial(kernel, tok_count, head_count), out_shap...]
where the time goes in v4:
time: 25.6 us; the launch traced here: 25.5 us
  Pallas kernels  24.8 us (97%)
  between operations  0.64 us (2%)
    pallas_call x1, Pallas kernels, per_device(): pl.pallas_call(functools.partial(kernel, tok_count, head_count), out_shap...  23.4 us
    pallas_call x1, Pallas kernels, per_device(): pl.pallas_call(place, out_shape=tuple((jax.ShapeDtypeStruct(x.shape, f32)...  1.43 us

profile of v4, /device:TPU:120, one launch (start us, length us, event | category | flops | bytes accessed | tf_op | source)
XLA Modules:
  0.0 25.5 jit_solution(1153728637834677921)
XLA Ops:
  0.6 23.4 %shard_map.84 = (f32[256,1024]{1,0:T(8,128)S(1)}, f32[256,1024]{1,0:T(8,128)S(1)}, f32[256,128]{1,0:T(8,128)S(1)}, f32[256,128]{1,0:T(8,128)S(1)}) custom-call(f32[256,1024]{1,0:T(8,128)} %q_hbm.1, f32[256,128]{1,0:T(8,128)} %k_hbm.1, f32[256,128]{1,0:T(8,128)} %v_hbm.1, f32[256,1024]{1,0:T(8,128)} %g_hbm.1, s32[1,32]{1,0:T(1,128)} %bitcast.1), custom_call_target="tpu_custom_call" | custom-call | tf_op jit(solution)/shard_map/pallas_call | solution.py:433
  24.0 1.4 %shard_map.85 = (f32[256,1024]{1,0:T(8,128)}, f32[256,1024]{1,0:T(8,128)}, f32[256,128]{1,0:T(8,128)}, f32[256,128]{1,0:T(8,128)}) custom-call(f32[256,1024]{1,0:T(8,128)S(1)} %get-tuple-element.8.a, f32[256,1024]{1,0:T(8,128)S(1)} %get-tuple-element.9.b, f32[256,128]{1,0:T(8,128)S(1)} %get-tuple-element.10.c, f32[256,128]{1,0:T(8,128)S(1)} %get-tuple-element.11.d), custom_call_target="tpu_custom_call" | custom-call | tf_op jit(solution)/shard_map/pallas_call | solution.py:481

commit v5 on v4

--- a/solution.py
+++ b/solution.py
@@ -86,6 +86,9 @@
     vt,
     s_own,
     dp_own,
+    own_top,
+    own_sum,
+    own_dot,
     inverse,
     delta,
     pf,
@@ -115,6 +118,10 @@
     others = [lax.rem(head + j, head_count) for j in range(1, head_count)]
     mine = rank(head)
     above = [rank(h) > mine for h in others]
+    earlier_rank = head + jnp.where((tok == 1) & (head == 0), head_count, 0)
+    straight = [has_next & (h < mine) for h in others]
+    greeted = [has_prev & ((h > head) | ((tok == 1) & (h == 0))) for h in others]
+    relayed = [has_prev & (h > earlier_rank) for h in others]
 
     def total(flags):
         return sum(flag.astype(jnp.int32) for flag in flags)
@@ -126,7 +133,8 @@
 
     pl.when(has_next)(lambda: signal(barrier, nxt))
     pl.when(has_prev)(lambda: signal(barrier, prv))
-    for h, flag in zip(others, above):
+    for h, flag, flag_prev in zip(others, above, greeted):
+        pl.when(flag_prev)(functools.partial(signal, barrier, (prv[0], h)))
         pl.when(flag)(functools.partial(signal, barrier, (tok, h)))
 
     loads = [
@@ -159,13 +167,13 @@
     id_mine[...] = dot_nn(ids, jnp.where(spread, 1.0, 0.0).astype(bf16))
     id_got[head] = id_mine[...]
 
-    pl.semaphore_wait(barrier, head_count - 1 - total(above) + total([has_next, has_prev]))
-
-    def send_ids(device, i, src, slot):
+    pl.semaphore_wait(barrier, head_count - 1 - total(above) + total([has_next, has_prev, *straight]))
+
+    def send_ids(device, i, src, slot, sent=None):
         return pltpu.make_async_remote_copy(
             src_ref=src,
             dst_ref=id_got.at[slot],
-            send_sem=id_send_sem.at[i],
+            send_sem=id_send_sem.at[i if sent is None else sent],
             recv_sem=id_recv_sem.at[i],
             device_id=device,
             device_id_type=MESH,
@@ -174,6 +182,10 @@
     slot = head_count + head
     ids_next = send_ids(nxt, 0, id_mine, slot)
     ids_beside = [send_ids((tok, h), 1 + j, id_mine, head) for j, h in enumerate(others)]
+    ids_straight = [
+        send_ids((nxt[0], h), head_count + j, id_mine, slot, 2 * head_count + j)
+        for j, h in enumerate(others)
+    ]
     ids_on = [
         send_ids((tok, h), head_count + j, id_got.at[slot], slot) for j, h in enumerate(others)
     ]
@@ -197,6 +209,8 @@
     @pl.when(has_next)
     def _():
         ids_next.start()
+        for copy, flag in zip(ids_straight, straight):
+            pl.when(flag)(copy.start)
         send_k.start()
         send_v.start()
 
@@ -210,17 +224,20 @@
     def pack_k(k, base):
         a, b, c = parts3(k)
         kc[base : base + 2 * TILE] = lanes(a, a, b, b, c, a)
-        kt[:, base : base + 2 * TILE] = rows(*parts2(k.T))
 
     def pack_v(v, base):
         a, b = parts2(v)
         vc[base : base + 2 * TILE] = lanes(a, a, b, b)
+
+    def turn(k, v, base):
+        kt[:, base : base + 2 * TILE] = rows(*parts2(k.T))
         vt[:, base : base + 2 * TILE] = rows(*parts2(v.T))
 
     loads[1].wait()
     loads[2].wait()
     pack_k(k_own[...], 2 * TILE)
     pack_v(v_own[...], 2 * TILE)
+    turn(k_own[...], v_own[...], 2 * TILE)
     loads[3].wait()
     loads[4].wait()
 
@@ -260,9 +277,47 @@
     @pl.when(has_prev)
     def _():
         ids_next.wait_recv()
-        for copy in ids_on:
-            copy.start()
-
+        for copy, flag in zip(ids_on, relayed):
+            pl.when(flag)(copy.start)
+
+
+    lane_group = lax.broadcasted_iota(jnp.int32, (8, TILE), 1) // IDS
+    per_tile = TILE // IDS
+
+    def id_row(first):
+        row = id_got[first]
+        for j in range(1, per_tile):
+            row = jnp.where(lane_group == j, id_got[first + j], row)
+        return jnp.broadcast_to(row[0:1], (TILE, TILE))
+
+    for copy in ids_beside:
+        copy.wait_recv()
+    of_queries = [id_row(0), id_row(per_tile)]
+    causal = lax.broadcasted_iota(jnp.int32, (TILE, TILE), 0) <= lax.broadcasted_iota(
+        jnp.int32, (TILE, TILE), 1
+    )
+
+    def set_bias(t, j, allowed):
+        bias[t, j * TILE : (j + 1) * TILE] = jnp.where(allowed, 0.0, NEG)
+
+    for t in range(TASKS):
+        set_bias(t, 2, (of_queries[t].T == of_queries[t]) & causal)
+    set_bias(1, 1, of_queries[0].T == of_queries[1])
+
+    def own_weights(pair, _):
+        for t in range(TASKS):
+            kept = slice(t * TILE, (1 + 2 * t) * TILE)
+            b = bias[t, (2 - t) * TILE :]
+            s = s_own[pair, kept] + lanes(b, b)
+            top = jnp.max(s, axis=0, keepdims=True)
+            w = jnp.exp2(s - top)
+            s_own[pair, kept] = w
+            own_top[t, pair] = top
+            own_sum[t, pair] = jnp.sum(w, axis=0, keepdims=True)
+            own_dot[t, pair] = jnp.sum(w * dp_own[pair, kept], axis=0, keepdims=True)
+        return 0
+
+    lax.fori_loop(0, PAIRS, own_weights, 0, unroll=True)
 
     pl.when(has_prev)(send_k.wait_recv)
     pack_k(k_prev[...], 0)
@@ -278,49 +333,27 @@
 
     lax.fori_loop(0, PAIRS, earlier_scores, 0, unroll=True)
 
-    for copy in ids_beside:
-        copy.wait_recv()
-
     @pl.when(has_prev)
     def _():
         for copy in ids_on:
             copy.wait_recv()
 
-    lane_group = lax.broadcasted_iota(jnp.int32, (8, TILE), 1) // IDS
-    per_tile = TILE // IDS
-    wide = []
-    for first in (head_count, head_count + per_tile, 0, per_tile):
-        row = id_got[first]
-        for j in range(1, per_tile):
-            row = jnp.where(lane_group == j, id_got[first + j], row)
-        wide.append(jnp.broadcast_to(row[0:1], (TILE, TILE)))
-    causal = lax.broadcasted_iota(jnp.int32, (TILE, TILE), 0) <= lax.broadcasted_iota(
-        jnp.int32, (TILE, TILE), 1
-    )
-    for t in range(TASKS):
-        for j in range(3):
-            allowed = wide[t + j].T == wide[2 + t]
-            if j == 2:
-                allowed = allowed & causal
-            bias[t, j * TILE : (j + 1) * TILE] = jnp.where(allowed, 0.0, NEG)
+    of_keys = [id_row(head_count).T, id_row(head_count + per_tile).T]
+    set_bias(0, 0, of_keys[0] == of_queries[0])
+    set_bias(0, 1, of_keys[1] == of_queries[0])
+    set_bias(1, 0, of_keys[1] == of_queries[1])
 
     def probs(t, pair, _):
         before = slice(t * TILE, 2 * TILE)
         kept = slice(t * TILE, (1 + 2 * t) * TILE)
         ahead = (2 - t) * TILE
-        b = bias[t]
-        s_prev = pf[t, pair, :ahead] + lanes(b[:ahead], b[:ahead])
-        s_here = s_own[pair, kept] + lanes(b[ahead:], b[ahead:])
-        top = jnp.maximum(
-            jnp.max(s_prev, axis=0, keepdims=True), jnp.max(s_here, axis=0, keepdims=True)
-        )
+        b = bias[t, :ahead]
+        s_prev = pf[t, pair, :ahead] + lanes(b, b)
+        top = jnp.maximum(own_top[t, pair], jnp.max(s_prev, axis=0, keepdims=True))
         w_prev = jnp.exp2(s_prev - top)
-        w_here = jnp.exp2(s_here - top)
-        s_own[pair, kept] = w_here
-        inv = 1.0 / (
-            jnp.sum(w_prev, axis=0, keepdims=True) + jnp.sum(w_here, axis=0, keepdims=True)
-        )
-        inverse[t, pair] = inv
+        shrink = jnp.exp2(own_top[t, pair] - top)
+        inv = 1.0 / (jnp.sum(w_prev, axis=0, keepdims=True) + own_sum[t, pair] * shrink)
+        inverse[t, pair] = inv * shrink
         p = w_prev * inv
         pf[t, pair, :ahead] = p
         high, low = parts2(p)
@@ -343,10 +376,9 @@
         before = slice(t * TILE, 2 * TILE)
         kept = slice(t * TILE, (1 + 2 * t) * TILE)
         ahead = (2 - t) * TILE
-        of_own = jnp.sum(s_own[pair, kept] * dp_own[pair, kept], axis=0, keepdims=True)
         dp = dot_nt(vc[before], g_pack(t, pair))
         p = pf[t, pair, :ahead]
-        row_delta = of_own * inverse[t, pair] + jnp.sum(p * dp, axis=0, keepdims=True)
+        row_delta = own_dot[t, pair] * inverse[t, pair] + jnp.sum(p * dp, axis=0, keepdims=True)
         delta[t, pair] = row_delta
         high, low = parts2(p * (dp - row_delta))
         ds1[t, pair, :ahead] = high
@@ -360,6 +392,8 @@
         tile = slice(t * TILE, (t + 1) * TILE)
         gk_out[tile] = (acc_k[tile, :TILE] + acc_k[tile, TILE:]) * (1.0 / LOG2E)
         pl.when(has_prev)(send_gk[t].start)
+
+    turn(k_prev[...], v_prev[...], 0)
 
     def results(pair, _):
         for t in range(TASKS):
@@ -407,8 +441,10 @@
         copy.wait_send()
     for copy in (ids_next, send_k, send_v):
         pl.when(has_next)(copy.wait_send)
-    for copy in (*ids_on, *send_gk, *send_gv):
+    for copy in (*send_gk, *send_gv):
         pl.when(has_prev)(copy.wait_send)
+    for copy, flag in zip((*ids_on, *ids_straight), (*relayed, *straight)):
+        pl.when(flag)(copy.wait_send)
 
 
 def place(a, b, c, d, a_out, b_out, c_out, d_out, sem):
@@ -456,8 +492,7 @@
             V((2 * TILE, 2 * own), bf16),
             V((PAIRS, win, own), f32),
             V((PAIRS, win, own), f32),
-            V((TASKS, PAIRS, 1, own), f32),
-            V((TASKS, PAIRS, 1, own), f32),
+            *[V((TASKS, PAIRS, 1, own), f32) for _ in range(5)],
             V((TASKS, PAIRS, own, own), f32),
             *[V((TASKS, PAIRS, own, own), bf16) for _ in range(4)],
             V((2 * own, 2 * TILE), f32),
@@ -465,7 +500,7 @@
             pltpu.SemaphoreType.DMA((5,)),
             pltpu.SemaphoreType.DMA((6,)),
             pltpu.SemaphoreType.DMA((6,)),
-            pltpu.SemaphoreType.DMA((2 * head_count,)),
+            pltpu.SemaphoreType.DMA((3 * head_count,)),
             pltpu.SemaphoreType.DMA((2 * head_count,)),
             pltpu.SemaphoreType.REGULAR,
         ],

time: 25.6 us -> 25.3 us (0.988)
  the two profiles are of different devices: /device:TPU:120 before, /device:TPU:254 now
where the time goes in v5:
time: 25.3 us; the launch traced here: 25.2 us
  Pallas kernels  24.5 us (97%)
  between operations  0.64 us (3%)
    pallas_call x1, Pallas kernels, per_device(): pl.pallas_call(functools.partial(kernel, tok_count, head_count), out_shap...  23.1 us
    pallas_call x1, Pallas kernels, per_device(): pl.pallas_call(place, out_shape=tuple((jax.ShapeDtypeStruct(x.shape, f32)...  1.43 us

profile of v5, /device:TPU:254, one launch (start us, length us, event | category | flops | bytes accessed | tf_op | source)
XLA Modules:
  0.0 25.2 jit_solution(13406500162855515137)
XLA Ops:
  0.6 23.1 %shard_map.84 = (f32[256,1024]{1,0:T(8,128)S(1)}, f32[256,1024]{1,0:T(8,128)S(1)}, f32[256,128]{1,0:T(8,128)S(1)}, f32[256,128]{1,0:T(8,128)S(1)}) custom-call(f32[256,1024]{1,0:T(8,128)} %q_hbm.1, f32[256,128]{1,0:T(8,128)} %k_hbm.1, f32[256,128]{1,0:T(8,128)} %v_hbm.1, f32[256,1024]{1,0:T(8,128)} %g_hbm.1, s32[1,32]{1,0:T(1,128)} %bitcast.1), custom_call_target="tpu_custom_call" | custom-call | tf_op jit(solution)/shard_map/pallas_call | solution.py:469
  23.7 1.4 %shard_map.85 = (f32[256,1024]{1,0:T(8,128)}, f32[256,1024]{1,0:T(8,128)}, f32[256,128]{1,0:T(8,128)}, f32[256,128]{1,0:T(8,128)}) custom-call(f32[256,1024]{1,0:T(8,128)S(1)} %get-tuple-element.8.a, f32[256,1024]{1,0:T(8,128)S(1)} %get-tuple-element.9.b, f32[256,128]{1,0:T(8,128)S(1)} %get-tuple-element.10.c, f32[256,128]{1,0:T(8,128)S(1)} %get-tuple-element.11.d), custom_call_target="tpu_custom_call" | custom-call | tf_op jit(solution)/shard_map/pallas_call | solution.py:516

commit v6 on v5

--- a/solution.py
+++ b/solution.py
@@ -237,7 +237,6 @@
     loads[2].wait()
     pack_k(k_own[...], 2 * TILE)
     pack_v(v_own[...], 2 * TILE)
-    turn(k_own[...], v_own[...], 2 * TILE)
     loads[3].wait()
     loads[4].wait()
 
@@ -394,6 +393,7 @@
         pl.when(has_prev)(send_gk[t].start)
 
     turn(k_prev[...], v_prev[...], 0)
+    turn(k_own[...], v_own[...], 2 * TILE)
 
     def results(pair, _):
         for t in range(TASKS):

time: 25.3 us -> 25.3 us (level)
  no operation moved by 1% of the time
where the time goes in v6:
time: 25.3 us; the launch traced here: 25.2 us
  Pallas kernels  24.5 us (97%)
  between operations  0.64 us (3%)
    pallas_call x1, Pallas kernels, per_device(): pl.pallas_call(functools.partial(kernel, tok_count, head_count), out_shap...  23.1 us
    pallas_call x1, Pallas kernels, per_device(): pl.pallas_call(place, out_shape=tuple((jax.ShapeDtypeStruct(x.shape, f32)...  1.43 us

profile of v6, /device:TPU:254, one launch (start us, length us, event | category | flops | bytes accessed | tf_op | source)
XLA Modules:
  0.0 25.2 jit_solution(4808284663023756224)
XLA Ops:
  0.6 23.1 %shard_map.84 = (f32[256,1024]{1,0:T(8,128)S(1)}, f32[256,1024]{1,0:T(8,128)S(1)}, f32[256,128]{1,0:T(8,128)S(1)}, f32[256,128]{1,0:T(8,128)S(1)}) custom-call(f32[256,1024]{1,0:T(8,128)} %q_hbm.1, f32[256,128]{1,0:T(8,128)} %k_hbm.1, f32[256,128]{1,0:T(8,128)} %v_hbm.1, f32[256,1024]{1,0:T(8,128)} %g_hbm.1, s32[1,32]{1,0:T(1,128)} %bitcast.1), custom_call_target="tpu_custom_call" | custom-call | tf_op jit(solution)/shard_map/pallas_call | solution.py:469
  23.7 1.4 %shard_map.85 = (f32[256,1024]{1,0:T(8,128)}, f32[256,1024]{1,0:T(8,128)}, f32[256,128]{1,0:T(8,128)}, f32[256,128]{1,0:T(8,128)}) custom-call(f32[256,1024]{1,0:T(8,128)S(1)} %get-tuple-element.8.a, f32[256,1024]{1,0:T(8,128)S(1)} %get-tuple-element.9.b, f32[256,128]{1,0:T(8,128)S(1)} %get-tuple-element.10.c, f32[256,128]{1,0:T(8,128)S(1)} %get-tuple-element.11.d), custom_call_target="tpu_custom_call" | custom-call | tf_op jit(solution)/shard_map/pallas_call | solution.py:516
